TPU v7x, 32 devices: a whole 2x2x4 slice. The times are simulated.
32 devices in a mesh: dp: 8 (over z, y), fsdp: 4 (over x, core).
Axes of the slice: x: 2, y: 2, z: 4, core: 2. Of those that a mesh axis runs over, the one named last changes fastest.
Arguments:
- tokens: bfloat16 [16384, 768], P(('dp', 'fsdp')), may hold values from -6 to 6
- lengths: int32 [32], P(('dp', 'fsdp')), may hold values from 80 to 512, as said below
- cotangent: bfloat16 [16384, 768], P(('dp', 'fsdp')), may hold values from -6 to 6
- qkv_weight: float32 [768, 2304], P('dp', 'fsdp'), may hold values from -0.109375 to 0.109375
- out_weight: float32 [768, 768], P('dp', 'fsdp'), may hold values from -1.75 to 1.75
- fc_weight: float32 [768, 3072], P('dp', 'fsdp'), may hold values from -0.21875 to 0.21875
- proj_weight: float32 [3072, 768], P('dp', 'fsdp'), may hold values from -0.109375 to 0.109375
- vectors: float32 [768, 12], P('dp', 'fsdp'), as said below
- qkv_first: float32 [768, 2304], P('dp', 'fsdp'), may hold values from -0.00024414062 to 0.00024414062
- out_first: float32 [768, 768], P('dp', 'fsdp'), may hold values from -4.5776367e-05 to 4.5776367e-05
- fc_first: float32 [768, 3072], P('dp', 'fsdp'), may hold values from -0.00024414062 to 0.00024414062
- proj_first: float32 [3072, 768], P('dp', 'fsdp'), may hold values from -0.00024414062 to 0.00024414062
- vectors_first: float32 [768, 12], P('dp', 'fsdp'), may hold values from -0.00024414062 to 0.00024414062
- qkv_second: float32 [768, 2304], P('dp', 'fsdp'), may hold values from 4.2330406e-09 to 3.5275338e-08
- out_second: float32 [768, 768], P('dp', 'fsdp'), may hold values from 1.4110135e-10 to 1.1288108e-09
- fc_second: float32 [768, 3072], P('dp', 'fsdp'), may hold values from 4.2330406e-09 to 2.8220272e-08
- proj_second: float32 [3072, 768], P('dp', 'fsdp'), may hold values from 4.2330406e-09 to 2.8220272e-08
- vectors_second: float32 [768, 12], P('dp', 'fsdp'), may hold values from 7.055068e-09 to 4.2330406e-08
Outputs:
- output: bfloat16 [16384, 768], P(('dp', 'fsdp'))
- input_grad: bfloat16 [16384, 768], P(('dp', 'fsdp'))
- grad_norm: float32 [], replicated
- qkv_weight_new: float32 [768, 2304], P('dp', 'fsdp')
- out_weight_new: float32 [768, 768], P('dp', 'fsdp')
- fc_weight_new: float32 [768, 3072], P('dp', 'fsdp')
- proj_weight_new: float32 [3072, 768], P('dp', 'fsdp')
- vectors_new: float32 [768, 12], P('dp', 'fsdp')
- qkv_first_new: float32 [768, 2304], P('dp', 'fsdp')
- out_first_new: float32 [768, 768], P('dp', 'fsdp')
- fc_first_new: float32 [768, 3072], P('dp', 'fsdp')
- proj_first_new: float32 [3072, 768], P('dp', 'fsdp')
- vectors_first_new: float32 [768, 12], P('dp', 'fsdp')
- qkv_second_new: float32 [768, 2304], P('dp', 'fsdp')
- out_second_new: float32 [768, 768], P('dp', 'fsdp')
- fc_second_new: float32 [768, 3072], P('dp', 'fsdp')
- proj_second_new: float32 [3072, 768], P('dp', 'fsdp')
- vectors_second_new: float32 [768, 12], P('dp', 'fsdp')
Inputs may be any that keep to these rules, and one draw needn't show every extreme that they name: lengths[s] counts the leading slots of sequence s that hold real tokens; one sequence has exactly 512 and another exactly 80. `vectors`: columns 0 and 2 are positive.
All inputs are finite; a program needn't handle non-finite values.
Results may differ from a plain program's by a relative error of at most 0.013.
The roundings to bfloat16 on the way count: a program that leaves them out, or rounds other values in their place, can miss the bound.
Values may be sent and summed in bfloat16 or wider, within the bound.
No kernel may reach another device: no remote copies, remote signals or barrier semaphores. Data moves between devices by JAX's collectives and lax.ppermute only.
A program may use at most 192 MiB of HBM per device.

v0:
```python
import jax
import jax.numpy as jnp
from jax import lax
from jax.sharding import PartitionSpec as P

HEAD_DIM = 64
STEP = 10


beta_one = 0.9
beta_two = 0.95
clip_limit = 1.0
rate_matrix = 0.1
rate_vector = 1.0
decay_matrix = 0.1
gelu_coeff = 0.7978845608028654
cubic_coeff = 0.044715
neg_large = -1e30


def split_up(value, dim, length):
    shape = value.shape
    parts = value.reshape(*shape[:dim], length, shape[dim] // length, *shape[dim + 1 :])
    return jnp.moveaxis(parts, dim, 0)


def sent_and_summed(value, axis, dim):
    parts = split_up(value, dim, lax.axis_size(axis))
    arrived = lax.all_to_all(parts, axis, split_axis=0, concat_axis=0, tiled=True)
    return arrived.astype(jnp.float32).sum(axis=0)


def sent_together(arrays, axis, dim, along):
    ends, at = ([], 0)
    for a in arrays[:-1]:
        at += a.shape[along]
        ends.append(at)
    both = jnp.concatenate(arrays, axis=along)
    return tuple(jnp.split(sent_and_summed(both, axis, dim), ends, axis=along))


def normalize(values):
    average = jnp.mean(values, axis=-1, keepdims=True)
    centred = values - average
    spread = jnp.mean(centred * centred, axis=-1, keepdims=True)
    inverse = lax.rsqrt(spread + 1e-05)
    return (centred * inverse, inverse)


def norm_backward(grad_hidden, normed, inverse, gain):
    grad_normed = grad_hidden * gain
    mean_plain = jnp.mean(grad_normed, axis=-1, keepdims=True)
    mean_cross = jnp.mean(grad_normed * normed, axis=-1, keepdims=True)
    return inverse * (grad_normed - mean_plain - normed * mean_cross)


def gelu_tanh(values):
    inner_arg = gelu_coeff * (values + cubic_coeff * values * values * values)
    return 0.5 * values * (1.0 + jnp.tanh(inner_arg))


def gelu_slope(values):
    inner_arg = gelu_coeff * (values + cubic_coeff * values * values * values)
    tanh_value = jnp.tanh(inner_arg)
    return 0.5 * (1.0 + tanh_value) + 0.5 * values * (
        1.0 - tanh_value * tanh_value
    ) * gelu_coeff * (1.0 + 3.0 * cubic_coeff * values * values)


def head_scores(query_rows, key_rows, key_mask, score_scale):
    scores = (
        jnp.einsum("qd,kd->qk", query_rows, key_rows, preferred_element_type=jnp.float32)
        * score_scale
    )
    return jnp.where(key_mask, scores, neg_large)


def head_forward(query_rows, key_rows, value_rows, key_mask, score_scale):
    scores = head_scores(query_rows, key_rows, key_mask, score_scale)
    row_top = jnp.max(scores, axis=-1, keepdims=True)
    shifted_exp = jnp.exp(scores - row_top)
    row_total = jnp.sum(shifted_exp, axis=-1, keepdims=True)
    prob_rows = (shifted_exp / row_total).astype(jnp.bfloat16)
    head_out = jnp.einsum("qk,kd->qd", prob_rows, value_rows, preferred_element_type=jnp.float32)
    return (head_out, row_top[:, 0] + jnp.log(row_total[:, 0]))


def head_backward(query_rows, key_rows, value_rows, grad_out, log_total, key_mask, score_scale):
    scores = head_scores(query_rows, key_rows, key_mask, score_scale)
    prob_rows = jnp.exp(scores - log_total[:, None])
    grad_values = jnp.einsum(
        "qk,qd->kd", prob_rows.astype(jnp.bfloat16), grad_out, preferred_element_type=jnp.float32
    )
    grad_probs = jnp.einsum("qd,kd->qk", grad_out, value_rows, preferred_element_type=jnp.float32)
    inner_sum = jnp.sum(prob_rows * grad_probs, axis=-1, keepdims=True)
    grad_scores = (prob_rows * (grad_probs - inner_sum)).astype(jnp.bfloat16)
    grad_query = (
        jnp.einsum("qk,kd->qd", grad_scores, key_rows, preferred_element_type=jnp.float32)
        * score_scale
    )
    grad_keys = (
        jnp.einsum("qk,qd->kd", grad_scores, query_rows, preferred_element_type=jnp.float32)
        * score_scale
    )
    return (grad_query, grad_keys, grad_values)


def gather_forward(shards):
    by_cols = (
        lax.all_gather(shards[0], "fsdp", axis=1, tiled=True),
        lax.all_gather(shards[1], "fsdp", axis=1, tiled=True),
        lax.all_gather(shards[2], "fsdp", axis=1, tiled=True),
        lax.all_gather(shards[3], "fsdp", axis=1, tiled=True),
        lax.all_gather(shards[4], "fsdp", axis=1, tiled=True),
    )
    return (
        lax.all_gather(by_cols[0], "dp", axis=0, tiled=True),
        lax.all_gather(by_cols[1], "dp", axis=0, tiled=True),
        lax.all_gather(by_cols[2], "dp", axis=0, tiled=True),
        lax.all_gather(by_cols[3], "dp", axis=0, tiled=True),
        lax.all_gather(by_cols[4], "dp", axis=0, tiled=True),
    )


def gather_backward(shards):
    by_cols = (
        lax.all_gather(shards[0], "fsdp", axis=1, tiled=True),
        lax.all_gather(shards[1], "fsdp", axis=1, tiled=True),
        lax.all_gather(shards[2], "fsdp", axis=1, tiled=True),
        lax.all_gather(shards[3], "fsdp", axis=1, tiled=True),
        lax.all_gather(shards[4], "fsdp", axis=1, tiled=True),
    )
    return (
        lax.all_gather(by_cols[0], "dp", axis=0, tiled=True),
        lax.all_gather(by_cols[1], "dp", axis=0, tiled=True),
        lax.all_gather(by_cols[2], "dp", axis=0, tiled=True),
        lax.all_gather(by_cols[3], "dp", axis=0, tiled=True),
        lax.all_gather(by_cols[4], "dp", axis=0, tiled=True),
    )


def adam_update(weight, gradient, moment_one, moment_two, factor, step_rate, decay_rate):
    clipped = gradient * factor
    moment_one_new = beta_one * moment_one + (1.0 - beta_one) * clipped
    moment_two_new = beta_two * moment_two + (1.0 - beta_two) * clipped * clipped
    first_hat = moment_one_new / (1.0 - beta_one**STEP)
    second_hat = moment_two_new / (1.0 - beta_two**STEP)
    weight_new = weight - step_rate * (
        first_hat / (jnp.sqrt(second_hat) + 1e-08) + decay_rate * weight
    )
    return (weight_new, moment_one_new, moment_two_new)


def body(
    tokens,
    lengths,
    cotangent,
    qkv_weight,
    out_weight,
    fc_weight,
    proj_weight,
    vectors,
    qkv_first,
    out_first,
    fc_first,
    proj_first,
    vectors_first,
    qkv_second,
    out_second,
    fc_second,
    proj_second,
    vectors_second,
):
    masters = (qkv_weight, out_weight, fc_weight, proj_weight, vectors)
    rounded = tuple((piece.astype(jnp.bfloat16) for piece in masters))
    gathered = gather_forward(rounded)
    seq_len, model_width = tokens.shape
    head_count = model_width // HEAD_DIM
    score_scale = HEAD_DIM ** (-0.5)
    positions = jnp.arange(seq_len, dtype=jnp.int32)
    key_mask = (positions[None, :] <= positions[:, None]) & (positions[None, :] < lengths[0])
    vector_table = gathered[4].astype(jnp.float32)
    gain_one = vector_table[:, 0]
    shift_one = vector_table[:, 1]
    gain_two = vector_table[:, 2]
    shift_two = vector_table[:, 3]
    bias_q = vector_table[:, 4]
    bias_v = vector_table[:, 5]
    bias_out = vector_table[:, 6]
    bias_proj = vector_table[:, 7]
    bias_fc = jnp.transpose(vector_table[:, 8:]).reshape(-1)
    resid_one = tokens.astype(jnp.float32)
    normed_one, inverse_one = normalize(resid_one)
    act_one = (normed_one * gain_one + shift_one).astype(jnp.bfloat16)
    bias_qkv = jnp.concatenate([bias_q, jnp.zeros_like(bias_q), bias_v])
    qkv_low = (jnp.dot(act_one, gathered[0], preferred_element_type=jnp.float32) + bias_qkv).astype(
        jnp.bfloat16
    )
    head_parts = qkv_low.reshape(seq_len, 3, head_count, HEAD_DIM).transpose(1, 2, 0, 3)

    def forward_head(operands):
        return head_forward(operands[0], operands[1], operands[2], key_mask, score_scale)

    head_out, log_totals = lax.map(forward_head, (head_parts[0], head_parts[1], head_parts[2]))
    mixed_low = head_out.transpose(1, 0, 2).reshape(seq_len, model_width).astype(jnp.bfloat16)
    resid_two = (
        resid_one + jnp.dot(mixed_low, gathered[1], preferred_element_type=jnp.float32) + bias_out
    )
    normed_two, inverse_two = normalize(resid_two)
    act_two = (normed_two * gain_two + shift_two).astype(jnp.bfloat16)
    pre_act = jnp.dot(act_two, gathered[2], preferred_element_type=jnp.float32) + bias_fc
    gelu_low = gelu_tanh(pre_act).astype(jnp.bfloat16)
    result = (
        resid_two + jnp.dot(gelu_low, gathered[3], preferred_element_type=jnp.float32) + bias_proj
    )
    output = result.astype(jnp.bfloat16)
    weights_back = gather_backward(rounded)
    grad_top = cotangent.astype(jnp.float32)
    g_bias_proj = jnp.sum(grad_top, axis=0)
    g_proj = jnp.einsum("tf,td->fd", gelu_low, cotangent, preferred_element_type=jnp.float32)
    grad_gelu = jnp.einsum(
        "td,fd->tf", cotangent, weights_back[3], preferred_element_type=jnp.float32
    )
    grad_pre = (grad_gelu * gelu_slope(pre_act)).astype(jnp.bfloat16)
    g_bias_fc = jnp.sum(grad_pre, axis=0, dtype=jnp.float32)
    g_fc = jnp.einsum("td,tf->df", act_two, grad_pre, preferred_element_type=jnp.float32)
    grad_act_two = jnp.einsum(
        "tf,df->td", grad_pre, weights_back[2], preferred_element_type=jnp.float32
    )
    g_gain_two = jnp.sum(grad_act_two * normed_two, axis=0)
    g_shift_two = jnp.sum(grad_act_two, axis=0)
    grad_resid_two = grad_top + norm_backward(grad_act_two, normed_two, inverse_two, gain_two)
    grad_branch = grad_resid_two.astype(jnp.bfloat16)
    g_bias_out = jnp.sum(grad_branch, axis=0, dtype=jnp.float32)
    g_out = jnp.einsum("td,te->de", mixed_low, grad_branch, preferred_element_type=jnp.float32)
    grad_mixed = jnp.einsum(
        "te,de->td", grad_branch, weights_back[1], preferred_element_type=jnp.float32
    ).astype(jnp.bfloat16)
    grad_heads = grad_mixed.reshape(seq_len, head_count, HEAD_DIM).transpose(1, 0, 2)

    def backward_head(operands):
        return head_backward(
            operands[0], operands[1], operands[2], operands[3], operands[4], key_mask, score_scale
        )

    grad_query, grad_keys, grad_values = lax.map(
        backward_head, (head_parts[0], head_parts[1], head_parts[2], grad_heads, log_totals)
    )
    grad_stack = jnp.stack([grad_query, grad_keys, grad_values]).transpose(2, 0, 1, 3)
    grad_qkv = grad_stack.reshape(seq_len, 3 * model_width).astype(jnp.bfloat16)
    g_bias_q = jnp.sum(grad_qkv[:, :model_width], axis=0, dtype=jnp.float32)
    g_bias_v = jnp.sum(grad_qkv[:, 2 * model_width :], axis=0, dtype=jnp.float32)
    g_qkv = jnp.einsum("td,te->de", act_one, grad_qkv, preferred_element_type=jnp.float32)
    grad_act_one = jnp.einsum(
        "te,de->td", grad_qkv, weights_back[0], preferred_element_type=jnp.float32
    )
    g_gain_one = jnp.sum(grad_act_one * normed_one, axis=0)
    g_shift_one = jnp.sum(grad_act_one, axis=0)
    input_grad = (
        grad_resid_two + norm_backward(grad_act_one, normed_one, inverse_one, gain_one)
    ).astype(jnp.bfloat16)
    small_columns = jnp.stack(
        [
            g_gain_one,
            g_shift_one,
            g_gain_two,
            g_shift_two,
            g_bias_q,
            g_bias_v,
            g_bias_out,
            g_bias_proj,
        ],
        axis=1,
    )
    grad_table = jnp.concatenate(
        [small_columns, jnp.transpose(g_bias_fc.reshape(-1, model_width))], axis=1
    )
    partly = (
        lax.psum_scatter(
            g_qkv.astype(jnp.bfloat16), "fsdp", scatter_dimension=1, tiled=True
        ).astype(jnp.float32),
        lax.psum_scatter(
            g_out.astype(jnp.bfloat16), "fsdp", scatter_dimension=1, tiled=True
        ).astype(jnp.float32),
        lax.psum_scatter(g_fc.astype(jnp.bfloat16), "fsdp", scatter_dimension=1, tiled=True).astype(
            jnp.float32
        ),
        lax.psum_scatter(
            g_proj.astype(jnp.bfloat16), "fsdp", scatter_dimension=1, tiled=True
        ).astype(jnp.float32),
        lax.psum_scatter(
            grad_table.astype(jnp.bfloat16), "fsdp", scatter_dimension=1, tiled=True
        ).astype(jnp.float32),
    )
    reduced = (
        *sent_together(
            (
                partly[0].astype(jnp.bfloat16),
                partly[1].astype(jnp.bfloat16),
                partly[2].astype(jnp.bfloat16),
            ),
            "dp",
            0,
            1,
        ),
        sent_and_summed(partly[3].astype(jnp.bfloat16), "dp", 0),
        sent_and_summed(partly[4].astype(jnp.bfloat16), "dp", 0),
    )
    local_squares = (
        jnp.sum(reduced[0] * reduced[0])
        + jnp.sum(reduced[1] * reduced[1])
        + jnp.sum(reduced[2] * reduced[2])
    )
    local_squares = (
        local_squares + jnp.sum(reduced[3] * reduced[3]) + jnp.sum(reduced[4] * reduced[4])
    )
    grad_norm = jnp.sqrt(lax.psum(local_squares, ("dp", "fsdp")))
    factor = jnp.minimum(1.0, clip_limit / (grad_norm + 1e-06))
    upd_qkv = adam_update(
        qkv_weight, reduced[0], qkv_first, qkv_second, factor, rate_matrix, decay_matrix
    )
    upd_out = adam_update(
        out_weight, reduced[1], out_first, out_second, factor, rate_matrix, decay_matrix
    )
    upd_fc = adam_update(
        fc_weight, reduced[2], fc_first, fc_second, factor, rate_matrix, decay_matrix
    )
    upd_proj = adam_update(
        proj_weight, reduced[3], proj_first, proj_second, factor, rate_matrix, decay_matrix
    )
    upd_vectors = adam_update(
        vectors, reduced[4], vectors_first, vectors_second, factor, rate_vector, 0.0
    )
    return (
        output,
        input_grad,
        grad_norm,
        upd_qkv[0],
        upd_out[0],
        upd_fc[0],
        upd_proj[0],
        upd_vectors[0],
        upd_qkv[1],
        upd_out[1],
        upd_fc[1],
        upd_proj[1],
        upd_vectors[1],
        upd_qkv[2],
        upd_out[2],
        upd_fc[2],
        upd_proj[2],
        upd_vectors[2],
    )


def solution(mesh):
    placed = (
        P(("dp", "fsdp"), None),
        P(("dp", "fsdp")),
        P(("dp", "fsdp"), None),
        P("dp", "fsdp"),
        P("dp", "fsdp"),
        P("dp", "fsdp"),
        P("dp", "fsdp"),
        P("dp", "fsdp"),
        P("dp", "fsdp"),
        P("dp", "fsdp"),
        P("dp", "fsdp"),
        P("dp", "fsdp"),
        P("dp", "fsdp"),
        P("dp", "fsdp"),
        P("dp", "fsdp"),
        P("dp", "fsdp"),
        P("dp", "fsdp"),
        P("dp", "fsdp"),
    )
    return jax.shard_map(
        body,
        mesh=mesh,
        in_specs=placed,
        out_specs=(
            P(("dp", "fsdp"), None),
            P(("dp", "fsdp"), None),
            P(),
            P("dp", "fsdp"),
            P("dp", "fsdp"),
            P("dp", "fsdp"),
            P("dp", "fsdp"),
            P("dp", "fsdp"),
            P("dp", "fsdp"),
            P("dp", "fsdp"),
            P("dp", "fsdp"),
            P("dp", "fsdp"),
            P("dp", "fsdp"),
            P("dp", "fsdp"),
            P("dp", "fsdp"),
            P("dp", "fsdp"),
            P("dp", "fsdp"),
            P("dp", "fsdp"),
        ),
        check_vma=False,
    )
```

profile of v0, /device:TPU:0, one launch (start us, length us, event | category | flops | bytes accessed | tf_op | source)
XLA Modules:
  0.0 631.6 jit_solution(4563172650528395452)
XLA Ops:
  8.2 8.6 %all-gather.2 = bf16[4,576,96]{1,2,0:T(8,128)(2,1)S(1)} all-gather(bf16[1,576,96]{1,2,0:T(8,128)(2,1)S(1)} %convert_bitcast_fusion.3), channel_id=1, replica_groups=mesh['dp'=8,'fsdp'=4] {'fsdp'}, dimensions={0}, use_global_device_ids=true | all-gather | bytes 552960 | tf_op jit(solution)/shard_map/all_gather | solution.py:110
  18.4 5.6 all_gather.42
  24.9 8.2 %all_gather.44 = bf16[96,3072]{1,0:T(8,128)(2,1)} all-gather(bf16[96,768]{1,0:T(8,128)(2,1)S(1)} %convert_element_type.131), channel_id=1, replica_groups=mesh['dp'=8,'fsdp'=4] {'fsdp'}, dimensions={1}, use_global_device_ids=true | all-gather | bytes 737280 | tf_op jit(solution)/shard_map/all_gather | solution.py:112
  33.3 8.1 %all_gather.46 = bf16[384,768]{0,1:T(8,128)(2,1)} all-gather(bf16[384,192]{0,1:T(8,128)(2,1)S(1)} %convert_element_type.133), channel_id=1, replica_groups=mesh['dp'=8,'fsdp'=4] {'fsdp'}, dimensions={1}, use_global_device_ids=true | all-gather | bytes 737280 | tf_op jit(solution)/shard_map/all_gather | solution.py:113
  41.5 5.1 all-gather
  46.6 31.2 %all-gather.1 = bf16[8,96,12]{1,2,0:T(8,128)(2,1)S(1)} all-gather(bf16[1,96,12]{1,2,0:T(8,128)(2,1)S(1)} %bitcast.182), channel_id=1, replica_groups=mesh['dp'=8,'fsdp'=4] {'dp'}, dimensions={0}, use_global_device_ids=true | all-gather | bytes 20736 | tf_op jit(solution)/shard_map/all_gather | solution.py:121
  79.3 5.7 all-gather.8.cloned.1.call-done
  84.9 5.6 fusion.55
  90.6 2.8 copy.96
  96.7 2.5 copy.98
  100.9 33.2 %while.28 = (s32[]{:T(128)}, bf16[12,512,64]{1,2,0:T(8,128)(2,1)S(1)}, f32[12,512]{1,0:T(8,128)S(1)}, bf16[12,512,64]{2,1,0:T(8,128)(2,1)S(1)}, bf16[12,512,64]{...) while((s32[]{:T(128)}, ...), condition=%wide.region_5.6_spmd.clone, body=%wide.region_2.5_spmd.clone.sunk | while | flops 69729792 | bytes 3693161 | solution.py:204
  135.4 2.3 fusion.88
  138.0 70.2 %all-gather.12.cloned.1.call-done = bf16[768,3072]{1,0:T(8,128)(2,1)} async-done(((bf16[96,3072]{1,0:T(8,128)(2,1)}), bf16[768,3072]{1,0:T(8,128)(2,1)}) %all-gather.12.cloned.1.call-update) | async-done | bytes 4718608 | tf_op jit(solution)/shard_map/all_gather | solution.py:119
  208.2 4.8 fusion.81
  213.0 2.7 copy-done.37
  215.6 5.0 convolution_convert_fusion.1
  220.9 68.4 %all-gather.14.cloned.1.call-done = bf16[3072,768]{0,1:T(8,128)(2,1)} async-done(((bf16[384,768]{0,1:T(8,128)(2,1)}), bf16[3072,768]{0,1:T(8,128)(2,1)}) %all-gather.14.cloned.1.call-update) | async-done | bytes 4718608 | tf_op jit(solution)/shard_map/all_gather | solution.py:120
  289.3 8.7 %fusion.89 = (bf16[3072]{0:T(1024)(128)(2,1)S(1)}, bf16[512,3072]{1,0:T(8,128)(2,1)S(1)}) fusion(f32[512,3072]{1,0:T(8,128)} %copy-done.37, f32[3072]{0:T(1024)S(1)} %add.235, bf16[512,768]{1,0:T(8,128)(2,1)} %param.24, bf16[3072,768]{0,1:T(8,128)(2,1)} %all-gather.14.cloned.1.call-done), kind=kOutput, calls=%fused_computation.175 | convolution fusion | flops 2448946176 | bytes 14960640 | tf_op jit(solution)/shard_map/td,fd->tf/dot_general | solution.py:221
  298.0 6.9 %multiply_reduce_fusion.1 = (bf16[768]{0:T(1024)(128)(2,1)S(1)}, f32[512]{0:T(512)S(1)}, f32[512]{0:T(512)S(1)}, bf16[768]{0:T(1024)(128)(2,1)S(1)}, f32[512,768]{1,0:T(8,128)S(1)}) fusion(f32[512,768]{1,0:T(8,128)S(1)} %get-tuple-element.301, f32[512]{0:T(512)S(1)} %add_rsqrt_fusion, f32[512]{0:T(512)S(1)} %broadcast_multiply_fusion.4, ...), kind=kOutput, calls=%fused_computation.97 | convolution fusion | flops 2419455488 | bytes 11024384 | tf_op jit(solution)/shard_map/tf,df->td/dot_general | solution.py:227
  304.9 2.3 convert_reduce_fusion.4
  308.9 2.5 copy.102
  315.3 91.6 %while.29 = (s32[]{:T(128)}, bf16[12,512,64]{1,2,0:T(8,128)(2,1)S(1)}, bf16[12,512,64]{1,2,0:T(8,128)(2,1)}, bf16[12,512,64]{1,2,0:T(8,128)(2,1)}, bf16[12,512,6...) while((s32[]{:T(128)}, ...), condition=%wide.region_12.13_spmd.clone, body=%wide.region_10.12_spmd.clone.sunk | while | flops 170720768 | bytes 9059961 | solution.py:246
  326.9 1.8 fusion.138
  342.2 1.8 fusion.138
  349.9 1.8 fusion.138
  357.5 1.8 fusion.138
  372.8 1.8 fusion.138
  388.1 1.8 fusion.138
  403.3 1.8 fusion.138
  409.9 4.1 convolution_convert_fusion
  414.3 7.7 %convolution_convert_fusion.2 = bf16[768,3072]{1,0:T(8,128)(2,1)} fusion(bf16[512,3072]{1,0:T(8,128)(2,1)} %copy-done.38, f32[512,768]{1,0:T(8,128)} %copy-done.3, f32[768]{0:T(1024)S(1)} %get-tuple-element.235, f32[768]{0:T(1024)S(1)} %get-tuple-element.233, f32[512]{0:T(512)S(1)} %add_rsqrt_fusion, f32[512]{0:T(512)S(1)} %broadcast_multiply_fusion.4), kind=kOutput, calls=%fused_computation.72 | convolution fusion | flops 2420244480 | bytes 9447424 | tf_op jit(solution)/shard_map/td,tf->df/dot_general | solution.py:226
  424.0 7.0 %fusion.69 = (bf16[768]{0:T(1024)(128)(2,1)S(1)}, f32[512]{0:T(512)}, f32[512]{0:T(512)}, bf16[768]{0:T(1024)(128)(2,1)S(1)}, f32[512,768]{1,0:T(8,128)}) fusion(bf16[512,768]{1,0:T(8,128)(2,1)S(1)} %copy-done, f32[512]{0:T(512)S(1)} %add_rsqrt_fusion.1, f32[512]{0:T(512)S(1)} %broadcast_multiply_fusion.5, f32[768]{0:T(1024)S(1)} %get-tuple-element.240, ...), kind=kOutput, calls=%fused_computation.94 | convolution fusion | flops 1815868928 | bytes 8271872 | tf_op jit(solution)/shard_map/te,de->td/dot_general | solution.py:254
  431.5 12.0 %all-reduce = bf16[768,12]{0,1:T(8,128)(2,1)S(1)} all-reduce(bf16[768,12]{0,1:T(8,128)(2,1)S(1)} %concatenate.12), channel_id=6, replica_groups=mesh['dp'=8,'fsdp'=4] {'fsdp'}, use_global_device_ids=true, to_apply=%region_34.35.clone | all-reduce | flops 9216 | bytes 36864
  444.2 3.6 all-to-all-start.2
  447.8 2.4 copy.115
  450.2 4.1 all-to-all-done.2
  454.3 3.6 all-to-all-start.1
  457.9 1.9 copy.108
  459.8 2.2 copy.107
  462.0 42.3 %reduce-scatter.9.cloned.1.call-done = bf16[768,768]{1,0:T(8,128)(2,1)} async-done(((bf16[768,3072]{1,0:T(8,128)(2,1)}), bf16[768,768]{1,0:T(8,128)(2,1)}) %reduce-scatter.9.cloned.1.call-update) | async-done | bytes 1179664 | tf_op jit(solution)/shard_map/reduce_scatter | solution.py:285
  504.3 4.9 concatenate.11
  509.2 5.8 all-to-all-start
  517.5 9.5 %add_convert_fusion = bf16[512,768]{1,0:T(8,128)(2,1)} fusion(f32[512,768]{1,0:T(8,128)} %copy-done.3, bf16[3072,768]{0,1:T(8,128)(2,1)} %all-gather.14.cloned.1.call-done, f32[768]{0:T(1024)S(1)} %get-tuple-element.234, f32[512,3072]{1,0:T(8,128)} %copy-done.37, f32[3072]{0:T(1024)} %copy-done.26), kind=kOutput, calls=%fused_computation.100 | convolution fusion | flops 2432827392 | bytes 13384704 | tf_op jit(solution)/shard_map/dot_general | solution.py:214
  529.2 39.7 %all-to-all-done = bf16[8,96,1536]{2,1,0:T(8,128)(2,1)} async-done(((bf16[8,96,1536]{2,1,0:T(8,128)(2,1)}), bf16[8,96,1536]{2,1,0:T(8,128)(2,1)}, u32[]{:S(2)}, u32[]{:S(2)}) %all-to-all-start) | async-done | bytes 2359328 | tf_op jit(solution)/shard_map/all_to_all | solution.py:29
  568.9 2.0 convert_reduce_fusion
  576.3 2.9 fusion.68
  579.2 37.6 %psum.7 = f32[]{:T(128)} all-reduce(f32[]{:T(128)S(6)} %add.251), channel_id=1, replica_groups=mesh['dp'=8,'fsdp'=4] {'dp','fsdp'}, use_global_device_ids=true, to_apply=%region_37.38 | all-reduce | flops 1 | bytes 8 | tf_op jit(solution)/shard_map/psum | solution.py:317
  617.6 1.9 multiply_subtract_fusion.2
  (299 shorter events, 144.0 us)
Async XLA Ops:
  7.2 77.8 %all-gather.8.cloned.1.call-start = ((), (), s32[]{:S(2)}) async-start(), calls=%async_computation.7 | async-start | bytes 3981312 | tf_op jit(solution)/shard_map/all_gather | solution.py:117
  8.2 10.1 %copy-start.15 = (f32[96,192]{1,0:T(8,128)S(1)}, f32[96,192]{1,0:T(8,128)}, u32[]{:S(2)}) copy-start(f32[96,192]{1,0:T(8,128)} %param.26) | copy-start | bytes 221188
  16.8 8.1 %copy-start.8 = (f32[96,768]{1,0:T(8,128)S(1)}, f32[96,768]{1,0:T(8,128)}, u32[]{:S(2)}) copy-start(f32[96,768]{1,0:T(8,128)} %param.27) | copy-start | bytes 884740
  18.2 15.1 %copy-start.10 = (f32[384,192]{0,1:T(8,128)S(1)}, f32[384,192]{0,1:T(8,128)}, u32[]{:S(2)}) copy-start(f32[384,192]{0,1:T(8,128)} %param.28) | copy-start | bytes 884740
  18.2 116.0 %all-gather.10.cloned.1.call-start = ((), (), s32[]{:S(2)}) async-start(), calls=%async_computation.8 | async-start | bytes 1327104 | tf_op jit(solution)/shard_map/all_gather | solution.py:118
  24.8 183.3 %all-gather.12.cloned.1.call-start = ((), (), s32[]{:S(2)}) async-start(), calls=%async_computation.9 | async-start | bytes 5308416 | tf_op jit(solution)/shard_map/all_gather | solution.py:119
  24.9 16.6 %copy-start.31 = (f32[96,3]{0,1:T(4,128)S(1)}, f32[96,3]{0,1:T(4,128)}, u32[]{:S(2)}) copy-start(f32[96,3]{0,1:T(4,128)} %param.29) | copy-start | bytes 3460
  24.9 53.0 %copy-start = (bf16[512,768]{1,0:T(8,128)(2,1)S(1)}, bf16[512,768]{1,0:T(8,128)(2,1)}, u32[]{:S(2)}) copy-start(bf16[512,768]{1,0:T(8,128)(2,1)} %param.22) | copy-start | bytes 2359300
  33.2 256.1 %all-gather.14.cloned.1.call-start = ((), (), s32[]{:S(2)}) async-start(), calls=%async_computation.10 | async-start | bytes 5308416 | tf_op jit(solution)/shard_map/all_gather | solution.py:120
  41.4 406.4 %reduce-scatter.11.cloned.1.call-start = ((), (), s32[]{:S(2)}) async-start(), calls=%async_computation.14 | async-start | bytes 5898240 | tf_op jit(solution)/shard_map/reduce_scatter | solution.py:288
  77.9 346.1 %copy-start.24 = (f32[768]{0:T(1024)}, f32[768]{0:T(1024)S(1)}, u32[]{:S(2)}) copy-start(f32[768]{0:T(1024)S(1)} %get-tuple-element.240) | copy-start | bytes 9220
  78.5 345.5 %copy-start.27 = (f32[512]{0:T(512)}, f32[512]{0:T(512)S(1)}, u32[]{:S(2)}) copy-start(f32[512]{0:T(512)S(1)} %add_rsqrt_fusion.1) | copy-start | bytes 6148
  79.2 210.1 %copy-start.26 = (f32[3072]{0:T(1024)}, f32[3072]{0:T(1024)S(1)}, u32[]{:S(2)}) copy-start(f32[3072]{0:T(1024)S(1)} %add.235) | copy-start | bytes 36868
  96.7 2.5 copy-start.5
  134.2 1.2 copy-start.4
  137.7 160.3 %copy-start.3 = (f32[512,768]{1,0:T(8,128)}, f32[512,768]{1,0:T(8,128)S(1)}, u32[]{:S(2)}) copy-start(f32[512,768]{1,0:T(8,128)S(1)} %get-tuple-element.301) | copy-start | bytes 4718596
  208.2 7.4 %copy-start.13 = (bf16[512,768]{1,0:T(8,128)(2,1)S(1)}, bf16[512,768]{1,0:T(8,128)(2,1)}, u32[]{:S(2)}) copy-start(bf16[512,768]{1,0:T(8,128)(2,1)} %param.24) | copy-start | bytes 2359300
  213.0 2.7 copy-start.37
  220.6 237.2 %reduce-scatter.7.cloned.1.call-start = ((), (), s32[]{:S(2)}) async-start(), calls=%async_computation.12 | async-start | bytes 1474560 | tf_op jit(solution)/shard_map/reduce_scatter | solution.py:282
  297.9 6.9 %copy-start.38 = (bf16[512,3072]{1,0:T(8,128)(2,1)}, bf16[512,3072]{1,0:T(8,128)(2,1)S(1)}, u32[]{:S(2)}) copy-start(bf16[512,3072]{1,0:T(8,128)(2,1)S(1)} %get-tuple-element.305) | copy-start | bytes 9437188
  298.0 6.9 %copy-start.14 = (bf16[512,768]{1,0:T(8,128)(2,1)S(1)}, bf16[512,768]{1,0:T(8,128)(2,1)}, u32[]{:S(2)}) copy-start(bf16[512,768]{1,0:T(8,128)(2,1)} %param.24) | copy-start | bytes 2359300
  304.9 2.3 copy-start.35
  313.2 146.5 %reduce-scatter.5.cloned.1.call-start = ((), (), s32[]{:S(2)}) async-start(), calls=%async_computation.11 | async-start | bytes 4423680 | tf_op jit(solution)/shard_map/reduce_scatter | solution.py:279
  408.5 1.4 copy-start.1
  414.1 90.2 %reduce-scatter.9.cloned.1.call-start = ((), (), s32[]{:S(2)}) async-start(), calls=%async_computation.13 | async-start | bytes 5898240 | tf_op jit(solution)/shard_map/reduce_scatter | solution.py:285
  424.0 7.0 %copy-start.2 = (bf16[3,12,512,64]{2,3,1,0:T(8,128)(2,1)S(1)}, bf16[3,12,512,64]{2,3,1,0:T(8,128)(2,1)}, u32[]{:S(2)}) copy-start(bf16[3,12,512,64]{2,3,1,0:T(8,128)(2,1)} %copy-done.1) | copy-start | bytes 7077892
  444.2 10.1 %all-to-all-start.2 = ((bf16[8,96,3]{1,2,0:T(4,128)(2,1)}), bf16[8,96,3]{1,2,0:T(4,128)(2,1)S(1)}, u32[]{:S(2)}, u32[]{:S(2)}) async-start(bf16[8,96,3]{1,2,0:T(4,128)(2,1)} %copy.110), calls=%async_computation.6 | async-start | bytes 16384 | tf_op jit(solution)/shard_map/all_to_all | solution.py:29
  454.3 54.9 %all-to-all-start.1 = ((bf16[8,384,192]{1,2,0:T(8,128)(2,1)}), bf16[8,384,192]{1,2,0:T(8,128)(2,1)S(1)}, u32[]{:S(2)}, u32[]{:S(2)}) async-start(bf16[8,384,192]{1,2,0:T(8,128)(2,1)} %bitcast.170), calls=%async_computation.5 | async-start | bytes 2359296 | tf_op jit(solution)/shard_map/all_to_all | solution.py:29
  509.2 59.7 %all-to-all-start = ((bf16[8,96,1536]{2,1,0:T(8,128)(2,1)}), bf16[8,96,1536]{2,1,0:T(8,128)(2,1)}, u32[]{:S(2)}, u32[]{:S(2)}) async-start(bf16[8,96,1536]{2,1,0:T(8,128)(2,1)} %bitcast.165), calls=%async_computation.3 | async-start | bytes 4718592 | tf_op jit(solution)/shard_map/all_to_all | solution.py:29
  529.2 47.0 %copy-start.25 = (f32[768]{0:T(1024)S(1)}, f32[768]{0:T(1024)}, u32[]{:S(2)}) copy-start(f32[768]{0:T(1024)} %copy-done.24) | copy-start | bytes 9220
  529.2 47.0 %copy-start.28 = (f32[512]{0:T(512)S(1)}, f32[512]{0:T(512)}, u32[]{:S(2)}) copy-start(f32[512]{0:T(512)} %copy-done.27) | copy-start | bytes 6148
  529.2 47.1 %copy-start.29 = (f32[512]{0:T(512)S(1)}, f32[512]{0:T(512)}, u32[]{:S(2)}) copy-start(f32[512]{0:T(512)} %broadcast_multiply_fusion) | copy-start | bytes 6148
  529.2 47.1 %copy-start.30 = (f32[512]{0:T(512)S(1)}, f32[512]{0:T(512)}, u32[]{:S(2)}) copy-start(f32[512]{0:T(512)} %broadcast_multiply_fusion.1) | copy-start | bytes 6148
  576.2 41.3 %copy-start.12 = (f32[96,576]{1,0:T(8,128)S(1)}, f32[96,576]{1,0:T(8,128)}, u32[]{:S(2)}) copy-start(f32[96,576]{1,0:T(8,128)} %param.25) | copy-start | bytes 663556
  576.2 41.3 %copy-start.21 = (f32[96,576]{1,0:T(8,128)S(1)}, f32[96,576]{1,0:T(8,128)}, u32[]{:S(2)}) copy-start(f32[96,576]{1,0:T(8,128)} %param.30) | copy-start | bytes 663556
  579.1 40.3 %copy-start.16 = (f32[96,192]{1,0:T(8,128)S(1)}, f32[96,192]{1,0:T(8,128)}, u32[]{:S(2)}) copy-start(f32[96,192]{1,0:T(8,128)} %param.26) | copy-start | bytes 221188
  579.1 40.3 %copy-start.22 = (f32[96,192]{1,0:T(8,128)S(1)}, f32[96,192]{1,0:T(8,128)}, u32[]{:S(2)}) copy-start(f32[96,192]{1,0:T(8,128)} %param.31) | copy-start | bytes 221188
  579.2 40.3 %copy-start.23 = (f32[96,192]{1,0:T(8,128)S(1)}, f32[96,192]{1,0:T(8,128)}, u32[]{:S(2)}) copy-start(f32[96,192]{1,0:T(8,128)} %param.36) | copy-start | bytes 221188
  579.2 41.2 %copy-start.9 = (f32[96,768]{1,0:T(8,128)S(1)}, f32[96,768]{1,0:T(8,128)}, u32[]{:S(2)}) copy-start(f32[96,768]{1,0:T(8,128)} %param.27) | copy-start | bytes 884740
  579.2 41.2 %copy-start.17 = (f32[96,768]{1,0:T(8,128)S(1)}, f32[96,768]{1,0:T(8,128)}, u32[]{:S(2)}) copy-start(f32[96,768]{1,0:T(8,128)} %param.32) | copy-start | bytes 884740
  579.2 41.2 %copy-start.18 = (f32[96,768]{1,0:T(8,128)S(1)}, f32[96,768]{1,0:T(8,128)}, u32[]{:S(2)}) copy-start(f32[96,768]{1,0:T(8,128)} %param.37) | copy-start | bytes 884740
  619.5 2.0 copy-start.7
  619.5 2.0 copy-start.11
  619.5 2.0 copy-start.19
  619.5 2.0 copy-start.20
  620.4 2.2 copy-start.32
  620.4 2.2 copy-start.33
  620.4 2.1 copy-start.34
  (2 other events, 1.4 us)
Sparse Core Ops, SparseCore 0:
  18.4 66.5 all-gather.7
  87.7 39.6 all-gather.9
  129.5 78.5 all-gather.11
  210.1 79.1 all-gather.13
  291.7 46.0 reduce-scatter.10
  340.3 25.7 reduce-scatter.6
  414.2 39.5 reduce-scatter.4
  456.5 47.7 reduce-scatter.8
where the time goes:
time: 643 us; the launch traced here: 632 us
  waiting for transfers between devices  231 us (36%)
  matrix products  183 us (28%)
  blocking collectives  116 us (18%)
  local copies, waits for them, and re-layouts  37.7 us (6%)
  other arithmetic  28.1 us (4%)
  between operations  21.7 us (3%)
  starting transfers between devices  13.7 us (2%)
    all_gather x1, waiting for transfers between devices, gather_forward(): lax.all_gather(by_cols[2], 'dp', axis=0, tiled=True)  70.2 us
    all_gather x1, waiting for transfers between devices, gather_forward(): lax.all_gather(by_cols[3], 'dp', axis=0, tiled=True)  68.4 us
    all_to_all x3, waiting for transfers between devices, sent_and_summed(): lax.all_to_all(parts, axis, split_axis=0, concat_axis=0, tiled=True)  43.8 us
    reduce_scatter x1, waiting for transfers between devices, body(): lax.psum_scatter(g_fc.astype(jnp.bfloat16), 'fsdp', scatter_dimension=1,...  42.3 us
    psum x1, blocking collectives, body(): grad_norm = jnp.sqrt(lax.psum(local_squares, ('dp', 'fsdp')))  37.6 us
    dot_general x24, matrix products, head_scores(): jnp.einsum('qd,kd->qk', query_rows, key_rows, preferred_element_type=jnp....  32.1 us
    all_gather x1, blocking collectives, gather_forward(): lax.all_gather(by_cols[4], 'dp', axis=0, tiled=True)  31.2 us
    dot_general x12, matrix products, head_backward(): jnp.einsum('qk,qd->kd', grad_scores, query_rows, preferred_element_type=j...  22 us
  transfers between devices with their start and end apart: 11, of which 6 were waited for; matrix products, arithmetic and copies ran while one was open for 36% of the time, Pallas kernels for 0%

commit v1 on v0

v1 whole, which is shorter than its diff:
```python
import functools

import jax
import jax.numpy as jnp
from jax import lax
from jax.experimental import pallas as pl
from jax.experimental.pallas import tpu as pltpu
from jax.sharding import PartitionSpec as P

HEAD_DIM = 64
STEP = 10

beta_one = 0.9
beta_two = 0.95
clip_limit = 1.0
rate_matrix = 0.1
rate_vector = 1.0
decay_matrix = 0.1
gelu_coeff = 0.7978845608028654
cubic_coeff = 0.044715
neg_large = -1e30
VEC_ROWS = 16

F32 = jnp.float32
BF16 = jnp.bfloat16
VMEM = pl.BlockSpec(memory_space=pltpu.VMEM)
ANY = pl.BlockSpec(memory_space=pl.ANY)
SMEM = pl.BlockSpec(memory_space=pltpu.SMEM)


def dot_nn(a, b):
    return lax.dot_general(a, b, (((1,), (0,)), ((), ())), preferred_element_type=F32)


def dot_nt(a, b):
    return lax.dot_general(a, b, (((1,), (1,)), ((), ())), preferred_element_type=F32)


def dot_tn(a, b):
    return lax.dot_general(a, b, (((0,), (0,)), ((), ())), preferred_element_type=F32)


def sds(shape, dtype):
    return jax.ShapeDtypeStruct(shape, dtype)


def call(body, ins, in_specs, outs, out_specs, scratch, flops, moved, limit):
    return pl.pallas_call(
        body,
        out_shape=outs,
        in_specs=in_specs,
        out_specs=out_specs,
        scratch_shapes=scratch,
        compiler_params=pltpu.CompilerParams(vmem_limit_bytes=limit << 20),
        cost_estimate=pl.CostEstimate(flops=flops, bytes_accessed=moved, transcendentals=0),
    )(*ins)


class Plan:
    def __init__(self, dp, fsdp, model, hidden):
        self.dp, self.fsdp = dp, fsdp
        self.sizes = {"x": fsdp // 2, "y": 2, "z": dp // 2}
        self.rows = model // dp
        self.cols = model // fsdp
        self.deep = hidden // dp
        self.direct = (
            dp % 2 == 0
            and fsdp % 2 == 0
            and self.rows % 32 == 0
            and self.cols % 32 == 0
            and self.deep % 128 == 0
        )

    def partner(self, value, stage, k):
        axis, step = {"x": ("fsdp", 2), "y": ("dp", 1), "z": ("dp", 2), "core": ("fsdp", 1)}[stage]
        n = self.dp if axis == "dp" else self.fsdp
        return lax.ppermute(value, axis, [(i, i ^ (step * k)) for i in range(n)])

    def blocks(self, order):
        out = []
        for x in range(self.sizes["x"]):
            for y in range(self.sizes["y"]):
                for z in range(self.sizes["z"]):
                    at, place, scale = {"x": x, "y": y, "z": z}, 0, 1
                    for s in order:
                        place += at[s] * scale
                        scale *= self.sizes[s]
                    out.append((place, 2 * z + y, 2 * x))
        return out

    def gather(self, value, order):
        held = value[None]
        for s in order:
            parts = [held] + [self.partner(held, s, k) for k in range(1, self.sizes[s])]
            held = jnp.concatenate(parts, axis=0)
        return held, self.partner(held, "core", 1)

    def scatter(self, own, away, order):
        arrived = self.partner(away, "core", 1)
        held, other = own, arrived
        for i, s in enumerate(reversed(order)):
            n = self.sizes[s]
            last = i == len(order) - 1
            shape = (n, held.shape[0] // n) + held.shape[1:]
            a, b = held.reshape(shape), other.reshape(shape)
            sums = [
                (a[k].astype(F32) + b[k].astype(F32)).astype(BF16) for k in list(range(1, n)) + [0]
            ]
            came = [self.partner(sums[k - 1], s, k) for k in range(1, n)]
            if last:
                return [sums[-1][0]] + [c[0] for c in came]
            held = sums[-1]
            if len(came) == 1:
                other = came[0]
            else:
                total = held.astype(F32)
                for c in came[:-1]:
                    total = total + c.astype(F32)
                held, other = total.astype(BF16), came[-1]


def block_copies(plan, order, half, place_of, me, piece, make):
    for core in range(2):
        for place, off_d, off_f in plan.blocks(order):
            make(piece[core], place, me[0] ^ off_d, me[1] ^ (off_f + core))


def pack_body(rows, deep, qkv, out, fc, proj, vec, a1, a2, b1, b2, c1, c2):
    half = rows // 2
    wide = qkv.shape[1]
    for ref, lo in ((a1, 0), (a2, half)):
        ref[0:half, 0:wide] = qkv[lo : lo + half, :].astype(BF16)
        ref[0:half, wide:] = out[lo : lo + half, :].astype(BF16)
    a1[half:, :] = jnp.zeros((VEC_ROWS, a1.shape[1]), BF16)
    eye = (
        lax.broadcasted_iota(jnp.int32, (rows, 128), 0)
        == lax.broadcasted_iota(jnp.int32, (rows, 128), 1)
    ).astype(BF16)
    turned = dot_tn(vec[...].astype(BF16), eye)
    a1[half : half + turned.shape[0], 0:128] = turned.astype(BF16)
    b1[...] = fc[0:half, :].astype(BF16)
    b2[...] = fc[half:, :].astype(BF16)
    flipped = jnp.transpose(proj[...]).astype(BF16)
    mid = flipped.shape[0] // 2
    c1[...] = flipped[:mid]
    c2[...] = flipped[mid:]


def normed(values):
    mean = jnp.mean(values, axis=-1, keepdims=True)
    centred = values - mean
    spread = jnp.mean(centred * centred, axis=-1, keepdims=True)
    inverse = lax.rsqrt(spread + 1e-05)
    return centred * inverse, inverse


def norm_back(grad_hidden, n, inverse, gain):
    g = grad_hidden * gain
    mean_plain = jnp.mean(g, axis=-1, keepdims=True)
    mean_cross = jnp.mean(g * n, axis=-1, keepdims=True)
    return inverse * (g - mean_plain - n * mean_cross)


class Table:
    def __init__(self, fsdp):
        self.per = 12 // fsdp

    def row(self, k):
        return (k // self.per) * VEC_ROWS + k % self.per

    def get(self, ref, k):
        r = self.row(k)
        return ref[r : r + 1, :]


def spread_matrix(rows, model, d):
    r = lax.broadcasted_iota(jnp.int32, (128, model), 0)
    c = lax.broadcasted_iota(jnp.int32, (128, model), 1)
    return ((c == r + d * rows) & (r < rows)).astype(BF16)


def front_body(plan, orders, n_in, me_ref, tokens, *refs):
    ins = refs[:n_in]
    qkv, act, a_out, t_out = refs[n_in : n_in + 4]
    a_v, vec_v, bias_v, sem, vec_sem, out_sem = refs[n_in + 4 :]
    fsdp, rows, half = plan.fsdp, plan.rows, plan.rows // 2
    model = a_v.shape[1]
    wide = qkv.shape[2]
    table = Table(fsdp)
    if plan.direct:
        me = (me_ref[0], me_ref[1])
        for h in range(2):

            def start(ref, place, d, f):
                at = pl.multiple_of(d * rows + h * half, 16)
                pltpu.make_async_copy(
                    ref.at[place, pl.ds(0, half), :], a_v.at[f, pl.ds(at, half), :], sem.at[f]
                ).start()
                if h == 0:
                    pltpu.make_async_copy(
                        ref.at[place, pl.ds(half, VEC_ROWS), pl.ds(0, 128)],
                        vec_v.at[d, pl.ds(pl.multiple_of(f * VEC_ROWS, 16), VEC_ROWS), :],
                        vec_sem,
                    ).start()

            block_copies(plan, orders[h], h, None, me, ins[2 * h : 2 * h + 2], start)
    else:
        for f in range(fsdp):
            pltpu.make_async_copy(ins[0].at[f], a_v.at[f], sem.at[f]).start()
    n, _ = normed(tokens[...].astype(F32))
    if plan.direct:
        pltpu.make_async_copy(vec_v, vec_v, vec_sem).wait()
        total = jnp.zeros(t_out.shape, F32)
        for d in range(plan.dp):
            total = total + dot_nn(vec_v[d], spread_matrix(rows, model, d))
        t_out[...] = total
    else:
        t_out[...] = ins[1][...]
    bias_v[:, 0:model] = jnp.broadcast_to(table.get(t_out, 4), (8, model))
    bias_v[:, model : 2 * model] = jnp.zeros((8, model), F32)
    bias_v[:, 2 * model :] = jnp.broadcast_to(table.get(t_out, 5), (8, model))
    act[...] = (n * table.get(t_out, 0) + table.get(t_out, 1)).astype(BF16)
    for f in range(fsdp):
        pltpu.make_async_copy(a_v.at[f], a_v.at[f], sem.at[f]).wait()
        pltpu.make_async_copy(a_v.at[f], a_out.at[f], out_sem.at[f]).start()
        r = dot_nn(act[...], a_v[f])[:, :wide] + bias_v[0:1, f * wide : (f + 1) * wide]
        qkv[f] = r.astype(BF16)
    for f in range(fsdp):
        pltpu.make_async_copy(a_v.at[f], a_out.at[f], out_sem.at[f]).wait()


def front(plan, orders, me, tokens, pieces, model, wide, cut):
    t = tokens.shape[0]
    fsdp = plan.fsdp
    full = wide + cut
    scratch = [
        pltpu.VMEM((fsdp, model, full), BF16),
        pltpu.VMEM((plan.dp if plan.direct else 1, fsdp * VEC_ROWS, 128), BF16),
        pltpu.VMEM((8, 3 * model), F32),
        pltpu.SemaphoreType.DMA((fsdp,)),
        pltpu.SemaphoreType.DMA,
        pltpu.SemaphoreType.DMA((fsdp,)),
    ]
    specs = [ANY] * len(pieces) if plan.direct else [ANY, VMEM]
    return call(
        functools.partial(front_body, plan, orders, len(pieces)),
        (me, tokens, *pieces),
        [SMEM, VMEM] + specs,
        (
            sds((fsdp, t, wide), BF16),
            sds((t, model), BF16),
            sds((fsdp, model, full), BF16),
            sds((fsdp * VEC_ROWS, model), F32),
        ),
        (VMEM, VMEM, ANY, VMEM),
        scratch,
        2 * t * model * 3 * model,
        12 << 20,
        48,
    )


def head_place(g, wide):
    return g // wide, g % wide


def masks(length, lo, size, keys):
    q = lax.broadcasted_iota(jnp.int32, (size, 1), 0) + lo
    limit = jnp.minimum(q, length - 1)
    k = lax.broadcasted_iota(jnp.int32, (size, keys), 1)
    return k <= limit


QBLOCK = 256


def attend_body(heads, wide, model, length_ref, qkv, mixed, logs):
    t = mixed.shape[0]
    length = length_ref[0]
    scale = HEAD_DIM**-0.5

    def part(h, which):
        f, o = head_place(which * model + h * HEAD_DIM, wide)
        return qkv[f, :, o : o + HEAD_DIM]

    for h in heads:
        q = part(h, 0) * jnp.asarray(scale, BF16)
        k, v = part(h, 1), part(h, 2)
        for lo in range(0, t, QBLOCK):
            n = lo + QBLOCK
            s = dot_nt(q[lo:n], k[:n])
            s = jnp.where(masks(length, lo, QBLOCK, n), s, neg_large)
            top = jnp.max(s, axis=-1, keepdims=True)
            e = jnp.exp(s - top)
            total = jnp.sum(e, axis=-1, keepdims=True)
            p = (e * (1.0 / total)).astype(BF16)
            o = dot_nn(p, v[:n])
            mixed[lo:n, h * HEAD_DIM : (h + 1) * HEAD_DIM] = o.astype(BF16)
            logs[lo:n, h : h + 1] = top + jnp.log(total)


def attend(qkv, length, model):
    fsdp, t, wide = qkv.shape
    heads = model // HEAD_DIM
    return call(
        functools.partial(attend_body, range(heads), wide, model),
        (length, qkv),
        [SMEM, VMEM],
        (sds((t, model), BF16), sds((t, 128), F32)),
        (VMEM, VMEM),
        [],
        4 * t * t * model,
        4 << 20,
        48,
    )


def join_body(table, wide, tokens, mixed, a_in, t_in, resid, act, wout):
    fsdp = a_in.shape[0]
    cut = a_in.shape[2] - wide
    for f in range(fsdp):
        wout[:, f * cut : (f + 1) * cut] = a_in[f, :, wide:]
    r = tokens[...].astype(F32) + dot_nn(mixed[...], wout[...]) + table.get(t_in, 6)
    resid[...] = r
    n, _ = normed(r)
    act[...] = (n * table.get(t_in, 2) + table.get(t_in, 3)).astype(BF16)


def join(plan, wide, tokens, mixed, a_can, t_can):
    t, model = tokens.shape
    return call(
        functools.partial(join_body, Table(plan.fsdp), wide),
        (tokens, mixed, a_can, t_can),
        [VMEM] * 4,
        (sds((t, model), F32), sds((t, model), BF16), sds((model, model), BF16)),
        (VMEM, VMEM, VMEM),
        [],
        2 * t * model * model,
        9 << 20,
        48,
    )


def grad_out_copies(plan, order, me, outs, slot_src, d, f, h, sem):
    off_d, off_f = d ^ me[0], f ^ me[1]
    at = {"x": off_f // 2, "y": off_d % 2, "z": off_d // 2}
    place, scale = 0, 1
    for s in order:
        place = place + at[s] * scale
        scale *= plan.sizes[s]
    core = off_f % 2
    for c in range(2):

        @pl.when(core == c)
        def _():
            pltpu.make_async_copy(slot_src, outs[2 * h + c].at[place], sem).start()


def mlp_body(plan, orders_b, orders_c, n_in, n_out, me_ref, act, cot, resid, t_in, *refs):
    ins, refs = refs[:n_in], refs[n_in:]
    output, gpre, b_out, g_b_fc, g_b_proj = refs[:5]
    gouts, refs = refs[5 : 5 + n_out], refs[5 + n_out :]
    b_v, c_v, acc, gp_v, sem, csem, osem, gsem = refs
    fsdp, rows, half = plan.fsdp, plan.rows, plan.rows // 2
    cols, chalf, deep = plan.cols, plan.cols // 2, plan.deep
    t, model = act.shape
    table = Table(fsdp)
    per = plan.dp // fsdp
    me = (me_ref[0], me_ref[1])
    if plan.direct:
        for h in range(2):

            def start_c(ref, place, d, f):
                pltpu.make_async_copy(
                    ref.at[place],
                    c_v.at[
                        pl.ds(pl.multiple_of(f * cols + h * chalf, 16), chalf),
                        pl.ds(pl.multiple_of(d * deep, 128), deep),
                    ],
                    csem.at[d // per],
                ).start()

            def start_b(ref, place, d, f):
                at = pl.multiple_of(d * rows + h * half, 16)
                pltpu.make_async_copy(
                    ref.at[place], b_v.at[f, pl.ds(at, half), :], sem.at[f]
                ).start()

            block_copies(plan, orders_b[h], h, None, me, ins[2 * h : 2 * h + 2], start_b)
            block_copies(plan, orders_c[h], h, None, me, ins[4 + 2 * h : 6 + 2 * h], start_c)
    else:
        for f in range(fsdp):
            pltpu.make_async_copy(ins[0].at[f], b_v.at[f], sem.at[f]).start()
            lanes = pl.ds(f * model, model)
            pltpu.make_async_copy(ins[1].at[:, lanes], c_v.at[:, lanes], csem.at[f]).start()
    acc[...] = resid[...] + table.get(t_in, 7)
    g_b_proj[...] = jnp.sum(cot[...].astype(F32), axis=0, keepdims=True)

    def drain(slot):
        pltpu.make_async_copy(gp_v.at[slot], gp_v.at[slot], gsem.at[slot]).wait()

    for j in range(fsdp):
        slot = j % 2
        lanes = pl.ds(j * model, model)
        pltpu.make_async_copy(b_v.at[j], b_v.at[j], sem.at[j]).wait()
        pltpu.make_async_copy(c_v.at[:, lanes], c_v.at[:, lanes], csem.at[j]).wait()
        pltpu.make_async_copy(b_v.at[j], b_out.at[j], osem.at[j]).start()
        pre = dot_nn(act[...], b_v[j]) + table.get(t_in, 8 + j)
        sq = pre * pre
        th = jnp.tanh(gelu_coeff * (pre + cubic_coeff * sq * pre))
        plus = 0.5 * (1.0 + th)
        gel = (pre * plus).astype(BF16)
        slope = plus + 0.5 * pre * (1.0 - th * th) * gelu_coeff * (1.0 + 3.0 * cubic_coeff * sq)
        acc[...] += dot_nt(gel, c_v[:, j * model : (j + 1) * model])
        gg = dot_nn(cot[...], c_v[:, j * model : (j + 1) * model]) * slope
        low = gg.astype(BF16)
        gpre[:, j * model : (j + 1) * model] = low
        g_b_fc[j : j + 1, :] = jnp.sum(low.astype(F32), axis=0, keepdims=True)
        if j >= 2:
            drain(slot)
        gp_v[slot] = dot_tn(cot[...], gel).astype(BF16)
        if plan.direct:
            for d in range(j * per, (j + 1) * per):
                for f in range(fsdp):
                    for h in range(2):
                        src = gp_v.at[
                            slot,
                            pl.ds(f * cols + h * chalf, chalf),
                            pl.ds((d - j * per) * deep, deep),
                        ]
                        grad_out_copies(plan, orders_c[h], me, gouts, src, d, f, h, gsem.at[slot])
        else:
            pltpu.make_async_copy(gp_v.at[slot], gouts[0].at[:, lanes], gsem.at[slot]).start()
    output[...] = acc[...].astype(BF16)
    drain(0)
    drain(1)
    for f in range(fsdp):
        pltpu.make_async_copy(b_v.at[f], b_out.at[f], osem.at[f]).wait()


def chunk_shapes(plan, rows, cols):
    n = plan.dp * plan.fsdp // 2
    return [sds((n, r, cols), BF16) for r in rows for _ in range(2)]


def mlp(plan, orders_b, orders_c, me, act, cot, resid, t_can, pieces, hidden):
    t, model = act.shape
    fsdp = plan.fsdp
    if plan.direct:
        grads = chunk_shapes(plan, [plan.cols // 2] * 2, plan.deep)
    else:
        grads = [sds((model, hidden), BF16)]
    return call(
        functools.partial(mlp_body, plan, orders_b, orders_c, len(pieces), len(grads)),
        (me, act, cot, resid, t_can, *pieces),
        [SMEM] + [VMEM] * 4 + [ANY] * len(pieces),
        (
            sds((t, model), BF16),
            sds((t, hidden), BF16),
            sds((fsdp, model, model), BF16),
            sds((fsdp, model), F32),
            sds((1, model), F32),
            *grads,
        ),
        (VMEM, VMEM, ANY, VMEM, VMEM) + (ANY,) * len(grads),
        [
            pltpu.VMEM((fsdp, model, model), BF16),
            pltpu.VMEM((model, hidden), BF16),
            pltpu.VMEM((t, model), F32),
            pltpu.VMEM((2, model, model), BF16),
            pltpu.SemaphoreType.DMA((fsdp,)),
            pltpu.SemaphoreType.DMA((fsdp,)),
            pltpu.SemaphoreType.DMA((fsdp,)),
            pltpu.SemaphoreType.DMA((2,)),
        ],
        8 * t * model * hidden,
        32 << 20,
        56,
    )


def mlp_back_body(plan, orders, n_out, me_ref, act, gpre, b_in, *refs):
    gact = refs[0]
    gouts = refs[1 : 1 + n_out]
    g_v, gsem = refs[1 + n_out :]
    fsdp, rows, half = plan.fsdp, plan.rows, plan.rows // 2
    model = act.shape[1]
    me = (me_ref[0], me_ref[1])

    def drain(slot):
        pltpu.make_async_copy(g_v.at[slot], g_v.at[slot], gsem.at[slot]).wait()

    for j in range(fsdp):
        slot = j % 2
        part = gpre[:, j * model : (j + 1) * model]
        if j >= 2:
            drain(slot)
        g_v[slot] = dot_tn(act[...], part).astype(BF16)
        if plan.direct:
            for d in range(plan.dp):
                for h in range(2):
                    src = g_v.at[slot, pl.ds(d * rows + h * half, half), :]
                    grad_out_copies(plan, orders[h], me, gouts, src, d, j, h, gsem.at[slot])
        else:
            pltpu.make_async_copy(g_v.at[slot], gouts[0].at[j], gsem.at[slot]).start()
        back = dot_nt(part, b_in[j])
        if j == 0:
            gact[...] = back
        else:
            gact[...] += back
    drain(0)
    drain(1)


def mlp_back(plan, orders, me, act, gpre, b_can):
    t, model = act.shape
    fsdp = plan.fsdp
    if plan.direct:
        grads = chunk_shapes(plan, [plan.rows // 2] * 2, model)
    else:
        grads = [sds((fsdp, model, model), BF16)]
    return call(
        functools.partial(mlp_back_body, plan, orders, len(grads)),
        (me, act, gpre, b_can),
        [SMEM] + [VMEM] * 3,
        (sds((t, model), F32), *grads),
        (VMEM,) + (ANY,) * len(grads),
        [pltpu.VMEM((2, model, model), BF16), pltpu.SemaphoreType.DMA((2,))],
        4 * t * model * gpre.shape[1],
        16 << 20,
        48,
    )


def join_back_body(table, gact, cot, resid, mixed, wout, t_in, gresid, gmixed, g_out, g_vec):
    n, inverse = normed(resid[...])
    e = gact[...]
    g_vec[...] = jnp.zeros(g_vec.shape, F32)
    g_vec[0:1, :] = jnp.sum(e * n, axis=0, keepdims=True)
    g_vec[1:2, :] = jnp.sum(e, axis=0, keepdims=True)
    r = cot[...].astype(F32) + norm_back(e, n, inverse, table.get(t_in, 2))
    gresid[...] = r
    branch = r.astype(BF16)
    g_vec[2:3, :] = jnp.sum(branch.astype(F32), axis=0, keepdims=True)
    gmixed[...] = dot_nt(branch, wout[...]).astype(BF16)
    g_out[...] = dot_tn(mixed[...], branch).astype(BF16)


def join_back(plan, gact, cot, resid, mixed, wout, t_can):
    t, model = cot.shape
    return call(
        functools.partial(join_back_body, Table(plan.fsdp)),
        (gact, cot, resid, mixed, wout, t_can),
        [VMEM] * 6,
        (
            sds((t, model), F32),
            sds((t, model), BF16),
            sds((model, model), BF16),
            sds((8, model), F32),
        ),
        (VMEM,) * 4,
        [],
        4 * t * model * model,
        10 << 20,
        48,
    )


def attend_back_body(heads, wide, model, length_ref, qkv, gmixed, logs, gqkv):
    t = gmixed.shape[0]
    length = length_ref[0]
    scale = HEAD_DIM**-0.5

    def put(h, which, lo, hi, value):
        f, o = head_place(which * model + h * HEAD_DIM, wide)
        gqkv[f, lo:hi, o : o + HEAD_DIM] = value.astype(BF16)

    def part(h, which):
        f, o = head_place(which * model + h * HEAD_DIM, wide)
        return qkv[f, :, o : o + HEAD_DIM]

    for h in heads:
        q = part(h, 0)
        small = q * jnp.asarray(scale, BF16)
        k, v = part(h, 1), part(h, 2)
        go = gmixed[:, h * HEAD_DIM : (h + 1) * HEAD_DIM]
        gk, gv = [], []
        for lo in range(0, t, QBLOCK):
            n = lo + QBLOCK
            s = dot_nt(small[lo:n], k[:n])
            s = jnp.where(masks(length, lo, QBLOCK, n), s, neg_large)
            p = jnp.exp(s - logs[lo:n, h : h + 1])
            gp = dot_nt(go[lo:n], v[:n])
            inner = jnp.sum(p * gp, axis=-1, keepdims=True)
            ds = (p * (gp - inner)).astype(BF16)
            put(h, 0, lo, n, dot_nn(ds, k[:n]) * scale)
            gv.append(dot_tn(p.astype(BF16), go[lo:n]))
            gk.append(dot_tn(ds, small[lo:n]))
        for b in range(t // QBLOCK):
            rows = slice(b * QBLOCK, (b + 1) * QBLOCK)
            put(h, 1, rows.start, rows.stop, sum(x[rows] for x in gk[b:]))
            put(h, 2, rows.start, rows.stop, sum(x[rows] for x in gv[b:]))


def attend_back(qkv, gmixed, logs, length):
    fsdp, t, wide = qkv.shape
    model = gmixed.shape[1]
    heads = model // HEAD_DIM
    return call(
        functools.partial(attend_back_body, range(heads), wide, model),
        (length, qkv, gmixed, logs),
        [SMEM] + [VMEM] * 3,
        sds(qkv.shape, BF16),
        VMEM,
        [],
        10 * t * t * model,
        6 << 20,
        48,
    )


def back_body(plan, orders, n_out, me_ref, tokens, act, gqkv, a_in, g_out, gresid, t_in, g_two, g_b_fc, g_b_proj, *refs):
    input_grad = refs[0]
    gouts = refs[1 : 1 + n_out]
    g_v, tab, vec_v, sum_v, gsem, vsem = refs[1 + n_out :]
    fsdp, rows, half = plan.fsdp, plan.rows, plan.rows // 2
    t, model = tokens.shape
    wide = gqkv.shape[2]
    cut = a_in.shape[2] - wide
    table = Table(fsdp)
    me = (me_ref[0], me_ref[1])
    back = jnp.zeros((t, model), F32)
    for f in range(fsdp):
        part = gqkv[f]
        g_v[f, :, 0:wide] = dot_tn(act[...], part).astype(BF16)
        g_v[f, :, wide:] = g_out[:, f * cut : (f + 1) * cut]
        if plan.direct:
            for d in range(plan.dp):
                for h in range(2):
                    src = g_v.at[f, pl.ds(d * rows + h * half, half), :]
                    if h == 0:
                        pieces = [r.at[:, pl.ds(0, half), :] for r in gouts[:2]]
                    else:
                        pieces = gouts[2:]
                    grad_out_copies(plan, orders[h], me, pieces, src, d, f, 0, gsem)
        else:
            pltpu.make_async_copy(g_v.at[f], gouts[0].at[f], gsem).start()
        sum_v[0:1, f * wide : (f + 1) * wide] = jnp.sum(part.astype(F32), axis=0, keepdims=True)
        back = back + dot_nt(part, a_in[f, :, :wide])
    n, inverse = normed(tokens[...].astype(F32))
    tab[...] = jnp.zeros(tab.shape, F32)

    def put(k, value):
        r = table.row(k)
        tab[r : r + 1, :] = value

    put(0, jnp.sum(back * n, axis=0, keepdims=True))
    put(1, jnp.sum(back, axis=0, keepdims=True))
    put(2, g_two[0:1, :])
    put(3, g_two[1:2, :])
    put(4, sum_v[0:1, 0:model])
    put(5, sum_v[0:1, 2 * model :])
    put(6, g_two[2:3, :])
    put(7, g_b_proj[...])
    for j in range(fsdp):
        put(8 + j, g_b_fc[j : j + 1, :])
    low = tab[...].astype(BF16)
    if plan.direct:
        vec_v[...] = jnp.zeros(vec_v.shape, BF16)
        for d in range(plan.dp):
            vec_v[d, :, 0:128] = dot_nt(low, spread_matrix(rows, model, d)).astype(BF16)
            for f in range(fsdp):
                src = vec_v.at[d, pl.ds(f * VEC_ROWS, VEC_ROWS), :]
                pieces = [r.at[:, pl.ds(half, VEC_ROWS), :] for r in gouts[:2]]
                grad_out_copies(plan, orders[0], me, pieces, src, d, f, 0, vsem)
    else:
        vec_v[0] = low
        pltpu.make_async_copy(vec_v.at[0], gouts[1], vsem).start()
    r = gresid[...] + norm_back(back, n, inverse, table.get(t_in, 0))
    input_grad[...] = r.astype(BF16)
    pltpu.make_async_copy(g_v, g_v, gsem).wait()
    pltpu.make_async_copy(vec_v, vec_v, vsem).wait()


def back_end(plan, orders, me, tokens, act, gqkv, a_can, g_out, gresid, t_can, g_two, g_b_fc, g_b_proj):
    t, model = tokens.shape
    fsdp, _, wide = gqkv.shape
    full = a_can.shape[2]
    half = plan.rows // 2
    if plan.direct:
        grads = chunk_shapes(plan, [half + VEC_ROWS, half], full)
    else:
        grads = [sds((fsdp, model, full), BF16), sds((fsdp * VEC_ROWS, model), BF16)]
    return call(
        functools.partial(back_body, plan, orders, len(grads)),
        (me, tokens, act, gqkv, a_can, g_out, gresid, t_can, g_two, g_b_fc, g_b_proj),
        [SMEM] + [VMEM] * 10,
        (sds((t, model), BF16), *grads),
        (VMEM,) + (ANY,) * len(grads),
        [
            pltpu.VMEM((fsdp, model, full), BF16),
            pltpu.VMEM((fsdp * VEC_ROWS, model), F32),
            pltpu.VMEM((plan.dp if plan.direct else 1, fsdp * VEC_ROWS, model), BF16),
            pltpu.VMEM((8, 3 * model), F32),
            pltpu.SemaphoreType.DMA,
            pltpu.SemaphoreType.DMA,
        ],
        4 * t * model * 3 * model,
        20 << 20,
        56,
    )


def total_of(refs):
    s = refs[0][...].astype(F32)
    for r in refs[1:]:
        s = s + r[...].astype(F32)
    return s


def finish_body(kind, wide, rows, per, counts, *refs):
    n = sum(counts)
    ins, outs = refs[:n], refs[n:]
    one, two = total_of(ins[: counts[0]]), total_of(ins[counts[0] :])
    square = outs[-1]
    if kind == "fc":
        half = rows // 2
        outs[0][0:half, :] = one
        outs[0][half:, :] = two
        total = jnp.sum(one * one) + jnp.sum(two * two)
    elif kind == "proj":
        both = jnp.concatenate([one, two], axis=0)
        outs[0][...] = jnp.transpose(both)
        total = jnp.sum(both * both)
    else:
        half = rows // 2
        turned = one[half : half + VEC_ROWS, 0:128]
        one = one[0:half]
        outs[0][0:half, :] = one[:, :wide]
        outs[0][half:, :] = two[:, :wide]
        outs[1][0:half, :] = one[:, wide:]
        outs[1][half:, :] = two[:, wide:]
        flat = jnp.transpose(turned)
        vec = flat[0:rows, 0:per]
        outs[2][...] = vec
        total = jnp.sum(one * one) + jnp.sum(two * two) + jnp.sum(vec * vec)
    square[...] = jnp.broadcast_to(total, square.shape)


def finish(kind, first, second, outs, wide, rows, per):
    outs = [sds(s, F32) for s in outs] + [sds((1, 128), F32)]
    ins = (*first, *second)
    return call(
        functools.partial(finish_body, kind, wide, rows, per, (len(first), len(second))),
        ins,
        [VMEM] * len(ins),
        tuple(outs),
        (VMEM,) * len(outs),
        [],
        1 << 20,
        2 << 20,
        16,
    )


def update_body(count, *refs):
    norms = refs[0]
    ins, outs = refs[1 : 1 + 4 * count], refs[1 + 4 * count :]
    norm = jnp.sqrt(jnp.sum(norms[...], axis=0, keepdims=True))
    outs[0][...] = norm
    factor = jnp.minimum(1.0, clip_limit / (norm[:, 0:1] + 1e-06))
    for i in range(count):
        w, g, one, two = (r[...] for r in ins[4 * i : 4 * i + 4])
        last = i == count - 1
        rate, decay = (rate_vector, 0.0) if last else (rate_matrix, decay_matrix)
        clipped = g * factor
        one_new = beta_one * one + (1.0 - beta_one) * clipped
        two_new = beta_two * two + (1.0 - beta_two) * clipped * clipped
        first_hat = one_new / (1.0 - beta_one**STEP)
        second_hat = two_new / (1.0 - beta_two**STEP)
        outs[1 + i][...] = w - rate * (first_hat / (jnp.sqrt(second_hat) + 1e-08) + decay * w)
        outs[1 + count + i][...] = one_new
        outs[1 + 2 * count + i][...] = two_new


def update(norms, weights, grads, firsts, seconds):
    count = len(weights)
    ins = [norms]
    for group in zip(weights, grads, firsts, seconds):
        ins += group
    outs = [sds((1, 128), F32)] + [sds(w.shape, F32) for w in weights] * 3
    return call(
        functools.partial(update_body, count),
        ins,
        [VMEM] * len(ins),
        tuple(outs),
        (VMEM,) * len(outs),
        [],
        4 << 20,
        6 << 20,
        32,
    )


def body(
    tokens,
    lengths,
    cotangent,
    qkv_weight,
    out_weight,
    fc_weight,
    proj_weight,
    vectors,
    qkv_first,
    out_first,
    fc_first,
    proj_first,
    vectors_first,
    qkv_second,
    out_second,
    fc_second,
    proj_second,
    vectors_second,
):
    dp, fsdp = lax.axis_size("dp"), lax.axis_size("fsdp")
    model = tokens.shape[1]
    wide, cut = qkv_weight.shape[1], out_weight.shape[1]
    hidden = fc_weight.shape[1] * fsdp
    per = vectors.shape[1]
    plan = Plan(dp, fsdp, model, hidden)
    rows, half = plan.rows, plan.rows // 2
    me = jnp.stack([lax.axis_index("dp"), lax.axis_index("fsdp")]).astype(jnp.int32)
    orders_a = (("z", "y", "x"), ("z", "x", "y"))
    orders_b = (("z", "y", "x"), ("z", "x", "y"))
    orders_c = (("y", "z", "x"), ("x", "z", "y"))

    if plan.direct:
        packed = call(
            functools.partial(pack_body, rows, plan.deep),
            (qkv_weight, out_weight, fc_weight, proj_weight, vectors),
            [VMEM] * 5,
            (
                sds((half + VEC_ROWS, wide + cut), BF16),
                sds((half, wide + cut), BF16),
                sds((half, model), BF16),
                sds((half, model), BF16),
                sds((plan.cols // 2, plan.deep), BF16),
                sds((plan.cols // 2, plan.deep), BF16),
            ),
            (VMEM,) * 6,
            [],
            1 << 20,
            2 << 20,
            16,
        )
        a_in = [r for h in range(2) for r in plan.gather(packed[h], orders_a[h])]
        b_in = [r for h in range(2) for r in plan.gather(packed[2 + h], orders_b[h])]
        c_in = [r for h in range(2) for r in plan.gather(packed[4 + h], orders_c[h])]
        bc_in = b_in + c_in
    else:

        def whole(shard):
            down = lax.all_gather(shard.astype(BF16), "dp", axis=0, tiled=True)
            return lax.all_gather(down, "fsdp", axis=0, tiled=False)

        a_all = whole(jnp.concatenate([qkv_weight, out_weight], axis=1))
        b_all = whole(fc_weight)
        c_all = jnp.transpose(whole(proj_weight), (0, 2, 1)).reshape(model, hidden)
        v_all = jnp.transpose(whole(vectors).astype(F32), (0, 2, 1))
        v_all = jnp.pad(v_all, ((0, 0), (0, VEC_ROWS - per), (0, 0)))
        a_in = [a_all, v_all.reshape(fsdp * VEC_ROWS, model)]
        bc_in = [b_all, c_all]

    qkv, act_one, a_can, t_can = front(plan, orders_a, me, tokens, a_in, model, wide, cut)
    mixed, logs = attend(qkv, lengths, model)
    resid_two, act_two, wout = join(plan, wide, tokens, mixed, a_can, t_can)
    output, gpre, b_can, g_b_fc, g_b_proj, *g_proj = mlp(
        plan, orders_b, orders_c, me, act_two, cotangent, resid_two, t_can, bc_in, hidden
    )
    gact, *g_fc = mlp_back(plan, orders_b, me, act_two, gpre, b_can)
    gresid, gmixed, g_out, g_two = join_back(
        plan, gact, cotangent, resid_two, mixed, wout, t_can
    )
    gqkv = attend_back(qkv, gmixed, logs, lengths)
    input_grad, *g_a = back_end(
        plan, orders_a, me, tokens, act_one, gqkv, a_can, g_out, gresid, t_can, g_two, g_b_fc, g_b_proj
    )

    if plan.direct:
        c_sum = [plan.scatter(g_proj[2 * h], g_proj[2 * h + 1], orders_c[h]) for h in range(2)]
        b_sum = [plan.scatter(g_fc[2 * h], g_fc[2 * h + 1], orders_b[h]) for h in range(2)]
        a_sum = [plan.scatter(g_a[2 * h], g_a[2 * h + 1], orders_a[h]) for h in range(2)]
        d_proj, s_c = finish("proj", c_sum[0], c_sum[1], [proj_weight.shape], wide, rows, per)
        d_fc, s_b = finish("fc", b_sum[0], b_sum[1], [fc_weight.shape], wide, rows, per)
        shapes = [qkv_weight.shape, out_weight.shape, vectors.shape]
        d_qkv, d_out, d_vec, s_a = finish("attention", a_sum[0], a_sum[1], shapes, wide, rows, per)
        squares = s_a + s_b + s_c
    else:

        def shared(value):
            mine = lax.psum_scatter(value, "fsdp", scatter_dimension=0, tiled=False)
            return lax.psum_scatter(mine, "dp", scatter_dimension=0, tiled=True).astype(F32)

        d_a = shared(g_a[0])
        d_qkv, d_out = d_a[:, :wide], d_a[:, wide:]
        d_fc = shared(g_fc[0])
        d_proj = shared(jnp.transpose(g_proj[0].reshape(fsdp, plan.cols, hidden), (0, 2, 1)))
        d_vec = shared(jnp.transpose(g_a[1].reshape(fsdp, VEC_ROWS, model)[:, :per], (0, 2, 1)))
        total = sum(jnp.sum(d * d) for d in (d_qkv, d_out, d_fc, d_proj, d_vec))
        squares = jnp.full((1, 128), total)

    sent = jnp.broadcast_to(squares[None], (dp * fsdp, 1, 128))
    norms = lax.all_to_all(sent, ("dp", "fsdp"), 0, 0, tiled=True).reshape(dp * fsdp, 128)
    result = update(
        norms,
        (qkv_weight, out_weight, fc_weight, proj_weight, vectors),
        (d_qkv, d_out, d_fc, d_proj, d_vec),
        (qkv_first, out_first, fc_first, proj_first, vectors_first),
        (qkv_second, out_second, fc_second, proj_second, vectors_second),
    )
    return (output, input_grad, result[0][0, 0], *result[1:])


def solution(mesh):
    tokens = P(("dp", "fsdp"), None)
    table = P("dp", "fsdp")
    return jax.shard_map(
        body,
        mesh=mesh,
        in_specs=(tokens, P(("dp", "fsdp")), tokens) + (table,) * 15,
        out_specs=(tokens, tokens, P()) + (table,) * 15,
        check_vma=False,
    )
```

time: 643 us -> 364 us (0.57); the launches traced: 632 us -> 359 us
  matrix products: 183 us -> 0 us
  waiting for transfers between devices: 231 us -> 102 us
  blocking collectives: 116 us -> 0 us
  Pallas kernels: 0 us -> 103 us
  starting transfers between devices: 13.7 us -> 93.5 us
  other arithmetic: 28.1 us -> 6.25 us
  between operations: 21.7 us -> 2.46 us
  local copies, waits for them, and re-layouts: 37.7 us -> 52.3 us
    dot_general x96 -> x0, matrix products: 183 us -> none  [the longest x24 32.1 us: head_scores(): jnp.einsum('qd,kd->qk', query_rows, key_rows, preferred_element_type=jnp....]
    all_gather x4 -> x0, waiting for transfers between devices: 144 us -> none  [the longest x1 70.2 us: gather_forward(): lax.all_gather(by_cols[2], 'dp', axis=0, tiled=True)]
    pallas_call x0 -> x13, Pallas kernels: none -> 103 us  [call(): pl.pallas_call(body, out_shape=outs, in_specs=in_specs, out_specs=out_spe...]
    ppermute x0 -> x72, waiting for transfers between devices: none -> 95 us  [partner(): return lax.ppermute(value, axis, [(i, i ^ step * k) for i in range(n)])]
    ppermute x0 -> x72, starting transfers between devices: none -> 89.7 us  [partner(): return lax.ppermute(value, axis, [(i, i ^ step * k) for i in range(n)])]
    all_gather x6 -> x0, blocking collectives: 66.8 us -> none  [the longest x1 31.2 us: gather_forward(): lax.all_gather(by_cols[4], 'dp', axis=0, tiled=True)]
    reduce_scatter x4 -> x0, waiting for transfers between devices: 42.4 us -> none  [the longest x1 42.3 us: body(): lax.psum_scatter(g_fc.astype(jnp.bfloat16), 'fsdp', scatter_dimension=1,...]
    psum x1 -> x0, blocking collectives: 37.6 us -> none  [body(): grad_norm = jnp.sqrt(lax.psum(local_squares, ('dp', 'fsdp')))]
  transfers between devices with their start and end apart: 11 -> 73, of which waited for: 6 -> 24; matrix products, arithmetic and copies ran while one was open for 36% -> 7% of each run, Pallas kernels for 0% -> 17%
where the time goes in v1:
time: 364 us; the launch traced here: 359 us
  Pallas kernels  103 us (28%)
  waiting for transfers between devices  102 us (28%)
  starting transfers between devices  93.5 us (26%)
  local copies, waits for them, and re-layouts  52.3 us (14%)
  other arithmetic  6.25 us (2%)
    pallas_call x13, Pallas kernels, call(): pl.pallas_call(body, out_shape=outs, in_specs=in_specs, out_specs=out_spe...  103 us
    ppermute x72, waiting for transfers between devices, partner(): return lax.ppermute(value, axis, [(i, i ^ step * k) for i in range(n)])  95 us
    ppermute x72, starting transfers between devices, partner(): return lax.ppermute(value, axis, [(i, i ^ step * k) for i in range(n)])  89.7 us
    unnamed x138, local copies, waits for them, and re-layouts  44.9 us
  transfers between devices with their start and end apart: 73, of which 24 were waited for; matrix products, arithmetic and copies ran while one was open for 7% of the time, Pallas kernels for 17%

profile of v1, /device:TPU:0, one launch (start us, length us, event | category | flops | bytes accessed | tf_op | source)
XLA Modules:
  0.0 359.2 jit_solution(10035165757866361505)
XLA Ops:
  5.5 3.1 collective-permute-start.18
  8.6 2.6 collective-permute-start.19
  11.2 1.7 collective-permute-start.30
  17.3 3.4 collective-permute-start.13
  23.4 3.6 %collective-permute-start.7 = (bf16[1,48,768]{2,1,0:T(8,128)(2,1)S(1)}, bf16[1,48,768]{2,1,0:T(8,128)(2,1)S(1)}, u32[]{:S(2)}, u32[]{:S(2)}) collective-permute-start(bf16[1,48,768]{2,1,0:T(8,128)(2,1)S(1)} %bitcast.56), channel_id=1, source_target_pairs={{0,16},{4,20},{8,24},{12,28},{16,0},{20,4},{24,8},{28,12},{1,17},{... | collective-permute-start | bytes 221192 | tf_op jit(solution)/shard_map/ppermute | solution.py:77
  29.6 3.8 %collective-permute-start.1 = (bf16[1,64,768]{2,1,0:T(8,128)(2,1)S(1)}, bf16[1,64,768]{2,1,0:T(8,128)(2,1)S(1)}, u32[]{:S(2)}, u32[]{:S(2)}) collective-permute-start(bf16[1,64,768]{2,1,0:T(8,128)(2,1)S(1)} %bitcast.52), channel_id=1, source_target_pairs={{0,16},{4,20},{8,24},{12,28},{16,0},{20,4},{24,8},{28,12},{1,17},{... | collective-permute-start | bytes 294920 | tf_op jit(solution)/shard_map/ppermute | solution.py:77
  35.4 3.8 %collective-permute-start.32 = (bf16[2,96,384]{2,1,0:T(8,128)(2,1)S(1)}, bf16[2,96,384]{2,1,0:T(8,128)(2,1)S(1)}, u32[]{:S(2)}, u32[]{:S(2)}) collective-permute-start(bf16[2,96,384]{2,1,0:T(8,128)(2,1)S(1)} %pad_maximum_fusion.5), channel_id=1, source_target_pairs={{0,16},{4,20},{8,24},{12,28},{16,0},{20,4},{24,8},{28,12},{1,17},{... | collective-permute-start | bytes 442376 | tf_op jit(solution)/shard_map/ppermute | solution.py:77
  40.7 2.1 collective-permute-done.1
  43.4 1.7 collective-permute-start.3
  45.2 5.9 %collective-permute-start.25 = (bf16[2,96,384]{2,1,0:T(8,128)(2,1)S(1)}, bf16[2,96,384]{2,1,0:T(8,128)(2,1)S(1)}, u32[]{:S(2)}, u32[]{:S(2)}) collective-permute-start(bf16[2,96,384]{2,1,0:T(8,128)(2,1)S(1)} %pad_maximum_fusion.4), channel_id=1, source_target_pairs={{0,8},{4,12},{8,0},{12,4},{16,24},{20,28},{24,16},{28,20},{1,9},{5... | collective-permute-start | bytes 442376 | tf_op jit(solution)/shard_map/ppermute | solution.py:77
  52.0 1.8 collective-permute-done.32
  60.9 4.0 %collective-permute-done.26 = bf16[2,96,384]{2,1,0:T(8,128)(2,1)S(1)} collective-permute-done((bf16[2,96,384]{2,1,0:T(8,128)(2,1)S(1)}, bf16[2,96,384]{2,1,0:T(8,128)(2,1)S(1)}, u32[]{:S(2)}, u32[]{:S(2)}) %collective-permute-start.26) | collective-permute-done | bytes 147488 | tf_op jit(solution)/shard_map/ppermute | solution.py:77
  66.8 1.9 collective-permute-done.10
  70.6 10.9 %collective-permute-done.21 = bf16[4,48,768]{2,1,0:T(8,128)(2,1)S(1)} collective-permute-done((bf16[4,48,768]{2,1,0:T(8,128)(2,1)S(1)}, bf16[4,48,768]{2,1,0:T(8,128)(2,1)S(1)}, u32[]{:S(2)}, u32[]{:S(2)}) %collective-permute-start.21) | collective-permute-done | bytes 294944 | tf_op jit(solution)/shard_map/ppermute | solution.py:77
  88.5 9.3 %collective-permute-done.28 = bf16[8,96,384]{2,1,0:T(8,128)(2,1)S(1)} collective-permute-done((bf16[8,96,384]{2,1,0:T(8,128)(2,1)S(1)}, bf16[8,96,384]{2,1,0:T(8,128)(2,1)S(1)}, u32[]{:S(2)}, u32[]{:S(2)}) %collective-permute-start.28) | collective-permute-done | bytes 589856 | tf_op jit(solution)/shard_map/ppermute | solution.py:77
  100.1 6.5 %collective-permute-done.16 = bf16[8,48,768]{2,1,0:T(8,128)(2,1)S(1)} collective-permute-done((bf16[8,48,768]{2,1,0:T(8,128)(2,1)S(1)}, bf16[8,48,768]{2,1,0:T(8,128)(2,1)S(1)}, u32[]{:S(2)}, u32[]{:S(2)}) %collective-permute-start.16) | collective-permute-done | bytes 589856 | tf_op jit(solution)/shard_map/ppermute | solution.py:77
  112.2 13.2 %shard_map.314 = (bf16[4,512,576]{2,1,0:T(8,128)(2,1)}, bf16[512,768]{1,0:T(8,128)(2,1)S(1)}, bf16[4,768,768]{2,1,0:T(8,128)(2,1)}, f32[64,768]{1,0:T(8,128)S(1)}) custom-call(s32[2]{0:T(128)S(1)} %pad_add_fusion.me_ref, bf16[512,768]{1,0:T(8,128)(2,1)S(1)} %copy-done.8, bf16[16,64,768]{2,1,0:T(8,128)(2,1)S(1)} %constant_dynamic-update-slice_fusion.5.refs_0_, ...), custom_call_target="tpu_custom_call" | custom-call | flops 1811939328 | bytes 12582912 | tf_op jit(solution)/shard_map/pallas_call | solution.py:48
  126.4 1.8 copy-done.41
  128.2 10.1 %shard_map.315 = (bf16[512,768]{1,0:T(8,128)(2,1)S(1)}, f32[512,128]{1,0:T(8,128)S(1)}) custom-call(s32[1]{0:T(128)S(6)} %copy.118.length_ref, bf16[4,512,576]{2,1,0:T(8,128)(2,1)S(1)} %copy-done.41), custom_call_target="tpu_custom_call" | custom-call | flops 805306368 | bytes 4194304 | tf_op jit(solution)/shard_map/pallas_call | solution.py:48
  138.3 4.2 %shard_map.316 = (f32[512,768]{1,0:T(8,128)S(1)}, bf16[512,768]{1,0:T(8,128)(2,1)S(1)}, bf16[768,768]{1,0:T(8,128)(2,1)S(1)}) custom-call(bf16[512,768]{1,0:T(8,128)(2,1)S(1)} %copy-done.8, bf16[512,768]{1,0:T(8,128)(2,1)S(1)} %get-tuple-element.83.mixed, bf16[4,768,768]{2,1,0:T(8,128)(2,1)} %get-tuple-element.84.a_in, f32[64,768]{1,0:T(8,128)S(1)} %get-tuple-element.85.t_in), custom_call_target="tpu_custom_call" | custom-call | flops 603979776 | bytes 9437184 | tf_op jit(solution)/shard_map/pallas_call | solution.py:48
  144.7 21.8 %shard_map.317 = (bf16[512,768]{1,0:T(8,128)(2,1)}, bf16[512,3072]{1,0:T(8,128)(2,1)}, bf16[4,768,768]{2,1,0:T(8,128)(2,1)}, f32[4,768]{1,0:T(4,128)}, f32[1,768...) custom-call(s32[2]{0:T(128)} %copy-done.39, ...), custom_call_target="tpu_custom_call" | custom-call | flops 9663676416 | bytes 33554432 | tf_op jit(solution)/shard_map/pallas_call | solution.py:48
  167.6 18.6 %shard_map.318 = (f32[512,768]{1,0:T(8,128)}, bf16[16,48,768]{2,1,0:T(8,128)(2,1)S(1)}, bf16[16,48,768]{2,1,0:T(8,128)(2,1)S(1)}, bf16[16,48,768]{2,1,0:T(8,128)(2,1)S(1)}, bf16[16,48,768]{2,1,0:T(8,128)(2,1)S(1)}) custom-call(s32[2]{0:T(128)S(1)} %copy-done.40, bf16[512,768]{1,0:T(8,128)(2,1)S(1)} %copy-done.37, bf16[512,3072]{1,0:T(8,128)(2,1)} %get-tuple-element.94.gpre, ...), custom_call_target="tpu_custom_call" | custom-call | flops 4831838208 | bytes 16777216 | tf_op jit(solution)/shard_map/pallas_call | solution.py:48
  186.7 4.4 %shard_map.319 = (f32[512,768]{1,0:T(8,128)}, bf16[512,768]{1,0:T(8,128)(2,1)S(1)}, bf16[768,768]{1,0:T(8,128)(2,1)S(1)}, f32[8,768]{1,0:T(8,128)S(1)}) custom-call(f32[512,768]{1,0:T(8,128)} %get-tuple-element.96.gact, bf16[512,768]{1,0:T(8,128)(2,1)S(1)} %copy-done.7, f32[512,768]{1,0:T(8,128)} %copy-done, bf16[512,768]{1,0:T(8,128)(2,1)S(1)} %get-tuple-element.83.mixed, ...), custom_call_target="tpu_custom_call" | custom-call | flops 1207959552 | bytes 10485760 | tf_op jit(solution)/shard_map/pallas_call | solution.py:48
  191.2 15.4 %shard_map.320.gqkv = bf16[4,512,576]{2,1,0:T(8,128)(2,1)S(1)} custom-call(s32[1]{0:T(128)S(6)} %copy.118.length_ref, bf16[4,512,576]{2,1,0:T(8,128)(2,1)} %get-tuple-element.82.qkv, bf16[512,768]{1,0:T(8,128)(2,1)S(1)} %get-tuple-element.98.gmixed, f32[512,128]{1,0:T(8,128)S(1)} %get-tuple-element.99.logs), custom_call_target="tpu_custom_call" | custom-call | flops 2013265920 | bytes 6291456 | tf_op jit(solution)/shard_map/pallas_call | solution.py:48
  208.2 12.7 %shard_map.321 = (bf16[512,768]{1,0:T(8,128)(2,1)}, bf16[16,64,768]{2,1,0:T(8,128)(2,1)}, bf16[16,64,768]{2,1,0:T(8,128)(2,1)}, bf16[16,48,768]{2,1,0:T(8,128)(2,1)}, bf16[16,48,768]{2,1,0:T(8,128)(2,1)}) custom-call(s32[2]{0:T(128)} %copy-done.39, bf16[512,768]{1,0:T(8,128)(2,1)} %tokens.5, bf16[512,768]{1,0:T(8,128)(2,1)} %copy-done.42, ...), custom_call_target="tpu_custom_call" | custom-call | flops 3623878656 | bytes 20971520 | tf_op jit(solution)/shard_map/pallas_call | solution.py:48
  232.2 7.6 %collective-permute-done.55 = bf16[8,48,768]{2,1,0:T(8,128)(2,1)S(1)} collective-permute-done((bf16[8,48,768]{2,1,0:T(8,128)(2,1)S(1)}, bf16[8,48,768]{2,1,0:T(8,128)(2,1)S(1)}, u32[]{:S(2)}, u32[]{:S(2)}) %collective-permute-start.55) | collective-permute-done | bytes 589856 | tf_op jit(solution)/shard_map/ppermute | solution.py:77
  242.9 21.2 %collective-permute-done.67 = bf16[8,96,384]{2,1,0:T(8,128)(2,1)S(1)} collective-permute-done((bf16[8,96,384]{2,1,0:T(8,128)(2,1)S(1)}, bf16[8,96,384]{2,1,0:T(8,128)(2,1)S(1)}, u32[]{:S(2)}, u32[]{:S(2)}) %collective-permute-start.67) | collective-permute-done | bytes 589856 | tf_op jit(solution)/shard_map/ppermute | solution.py:77
  265.6 2.2 collective-permute-start.69
  267.9 4.8 %collective-permute-done.68 = bf16[2,96,384]{2,1,0:T(8,128)(2,1)S(1)} collective-permute-done((bf16[2,96,384]{2,1,0:T(8,128)(2,1)S(1)}, bf16[2,96,384]{2,1,0:T(8,128)(2,1)S(1)}, u32[]{:S(2)}, u32[]{:S(2)}) %collective-permute-start.68) | collective-permute-done | bytes 147488 | tf_op jit(solution)/shard_map/ppermute | solution.py:77
  273.2 2.7 collective-permute-start.63
  276.0 4.7 %collective-permute-done.62 = bf16[2,96,384]{2,1,0:T(8,128)(2,1)S(1)} collective-permute-done((bf16[2,96,384]{2,1,0:T(8,128)(2,1)S(1)}, bf16[2,96,384]{2,1,0:T(8,128)(2,1)S(1)}, u32[]{:S(2)}, u32[]{:S(2)}) %collective-permute-start.62) | collective-permute-done | bytes 147488 | tf_op jit(solution)/shard_map/ppermute | solution.py:77
  281.7 4.7 %collective-permute-start.70 = (bf16[2,96,384]{2,1,0:T(8,128)(2,1)S(1)}, bf16[2,96,384]{2,1,0:T(8,128)(2,1)S(1)}, u32[]{:S(2)}, u32[]{:S(2)}) collective-permute-start(bf16[2,96,384]{2,1,0:T(8,128)(2,1)S(1)} %get-tuple-element.199), channel_id=1, source_target_pairs={{0,24},{4,28},{8,16},{12,20},{16,8},{20,12},{24,0},{28,4},{1,25},{... | collective-permute-start | bytes 442376 | tf_op jit(solution)/shard_map/ppermute | solution.py:77
  286.5 3.8 %collective-permute-done.70 = bf16[2,96,384]{2,1,0:T(8,128)(2,1)S(1)} collective-permute-done((bf16[2,96,384]{2,1,0:T(8,128)(2,1)S(1)}, bf16[2,96,384]{2,1,0:T(8,128)(2,1)S(1)}, u32[]{:S(2)}, u32[]{:S(2)}) %collective-permute-start.70) | collective-permute-done | bytes 147488 | tf_op jit(solution)/shard_map/ppermute | solution.py:77
  290.4 3.1 collective-permute-start.64
  293.5 4.0 %collective-permute-done.64 = bf16[2,96,384]{2,1,0:T(8,128)(2,1)S(1)} collective-permute-done((bf16[2,96,384]{2,1,0:T(8,128)(2,1)S(1)}, bf16[2,96,384]{2,1,0:T(8,128)(2,1)S(1)}, u32[]{:S(2)}, u32[]{:S(2)}) %collective-permute-start.64) | collective-permute-done | bytes 147488 | tf_op jit(solution)/shard_map/ppermute | solution.py:77
  297.6 3.9 %collective-permute-start.65 = (bf16[1,96,384]{2,1,0:T(8,128)(2,1)S(1)}, bf16[1,96,384]{2,1,0:T(8,128)(2,1)S(1)}, u32[]{:S(2)}, u32[]{:S(2)}) collective-permute-start(bf16[1,96,384]{2,1,0:T(8,128)(2,1)S(1)} %get-tuple-element.226), channel_id=1, source_target_pairs={{0,4},{4,0},{8,12},{12,8},{16,20},{20,16},{24,28},{28,24},{1,5},{5... | collective-permute-start | bytes 221192 | tf_op jit(solution)/shard_map/ppermute | solution.py:77
  302.1 2.6 collective-permute-start.58
  304.8 1.8 collective-permute-start.59
  306.7 1.7 collective-permute-done.57
  309.3 2.9 collective-permute-done.58
  312.3 4.4 %collective-permute-start.40 = (bf16[1,64,768]{2,1,0:T(8,128)(2,1)S(1)}, bf16[1,64,768]{2,1,0:T(8,128)(2,1)S(1)}, u32[]{:S(2)}, u32[]{:S(2)}) collective-permute-start(bf16[1,64,768]{2,1,0:T(8,128)(2,1)S(1)} %get-tuple-element.207), channel_id=1, source_target_pairs={{0,16},{4,20},{8,24},{12,28},{16,0},{20,4},{24,8},{28,12},{1,17},{... | collective-permute-start | bytes 294920 | tf_op jit(solution)/shard_map/ppermute | solution.py:77
  316.8 2.3 collective-permute-start.41
  319.0 2.1 collective-permute-start.46
  321.2 2.2 collective-permute-start.47
  324.6 1.8 collective-permute-done.46
  330.3 3.8 %all-to-all-start = ((f32[32,1,128]{2,1,0:T(1,128)}), f32[32,1,128]{2,1,0:T(1,128)S(1)}, u32[]{:S(2)}, u32[]{:S(2)}) async-start(f32[32,1,128]{2,1,0:T(1,128)} %broadcast_in_dim.33), calls=%async_computation | async-start | bytes 32768 | tf_op jit(solution)/shard_map/all_to_all | solution.py:913
  334.7 6.5 %all-to-all-done = f32[32,1,128]{2,1,0:T(1,128)S(1)} async-done(((f32[32,1,128]{2,1,0:T(1,128)}), f32[32,1,128]{2,1,0:T(1,128)S(1)}, u32[]{:S(2)}, u32[]{:S(2)}) %all-to-all-start) | async-done | bytes 16416 | tf_op jit(solution)/shard_map/all_to_all | solution.py:913
  350.4 1.9 shard_map.325
  (290 shorter events, 91.4 us)
Async XLA Ops:
  5.5 16.5 %collective-permute-start.18 = (bf16[1,48,768]{2,1,0:T(8,128)(2,1)S(1)}, bf16[1,48,768]{2,1,0:T(8,128)(2,1)S(1)}, u32[]{:S(2)}, u32[]{:S(2)}) collective-permute-start(bf16[1,48,768]{2,1,0:T(8,128)(2,1)S(1)} %bitcast.63), channel_id=1, source_target_pairs={{0,8},{4,12},{8,0},{12,4},{16,24},{20,28},{24,16},{28,20},{1,9},{5... | collective-permute-start | bytes 221192 | tf_op jit(solution)/shard_map/ppermute | solution.py:77
  8.6 14.2 %collective-permute-start.19 = (bf16[1,48,768]{2,1,0:T(8,128)(2,1)S(1)}, bf16[1,48,768]{2,1,0:T(8,128)(2,1)S(1)}, u32[]{:S(2)}, u32[]{:S(2)}) collective-permute-start(bf16[1,48,768]{2,1,0:T(8,128)(2,1)S(1)} %bitcast.64), channel_id=1, source_target_pairs={{0,16},{4,20},{8,24},{12,28},{16,0},{20,4},{24,8},{28,12},{1,17},{... | collective-permute-start | bytes 221192 | tf_op jit(solution)/shard_map/ppermute | solution.py:77
  11.2 12.2 %collective-permute-start.20 = (bf16[1,48,768]{2,1,0:T(8,128)(2,1)S(1)}, bf16[1,48,768]{2,1,0:T(8,128)(2,1)S(1)}, u32[]{:S(2)}, u32[]{:S(2)}) collective-permute-start(bf16[1,48,768]{2,1,0:T(8,128)(2,1)S(1)} %bitcast.65), channel_id=1, source_target_pairs={{0,24},{4,28},{8,16},{12,20},{16,8},{20,12},{24,0},{28,4},{1,25},{... | collective-permute-start | bytes 221192 | tf_op jit(solution)/shard_map/ppermute | solution.py:77
  16.4 11.9 %collective-permute-start.12 = (bf16[1,48,768]{2,1,0:T(8,128)(2,1)S(1)}, bf16[1,48,768]{2,1,0:T(8,128)(2,1)S(1)}, u32[]{:S(2)}, u32[]{:S(2)}) collective-permute-start(bf16[1,48,768]{2,1,0:T(8,128)(2,1)S(1)} %bitcast.59), channel_id=1, source_target_pairs={{0,8},{4,12},{8,0},{12,4},{16,24},{20,28},{24,16},{28,20},{1,9},{5... | collective-permute-start | bytes 221192 | tf_op jit(solution)/shard_map/ppermute | solution.py:77
  17.3 11.9 %collective-permute-start.13 = (bf16[1,48,768]{2,1,0:T(8,128)(2,1)S(1)}, bf16[1,48,768]{2,1,0:T(8,128)(2,1)S(1)}, u32[]{:S(2)}, u32[]{:S(2)}) collective-permute-start(bf16[1,48,768]{2,1,0:T(8,128)(2,1)S(1)} %bitcast.60), channel_id=1, source_target_pairs={{0,16},{4,20},{8,24},{12,28},{16,0},{20,4},{24,8},{28,12},{1,17},{... | collective-permute-start | bytes 221192 | tf_op jit(solution)/shard_map/ppermute | solution.py:77
  22.9 11.8 %collective-permute-start.6 = (bf16[1,48,768]{2,1,0:T(8,128)(2,1)S(1)}, bf16[1,48,768]{2,1,0:T(8,128)(2,1)S(1)}, u32[]{:S(2)}, u32[]{:S(2)}) collective-permute-start(bf16[1,48,768]{2,1,0:T(8,128)(2,1)S(1)} %bitcast.55), channel_id=1, source_target_pairs={{0,8},{4,12},{8,0},{12,4},{16,24},{20,28},{24,16},{28,20},{1,9},{5... | collective-permute-start | bytes 221192 | tf_op jit(solution)/shard_map/ppermute | solution.py:77
  23.4 11.6 %collective-permute-start.7 = (bf16[1,48,768]{2,1,0:T(8,128)(2,1)S(1)}, bf16[1,48,768]{2,1,0:T(8,128)(2,1)S(1)}, u32[]{:S(2)}, u32[]{:S(2)}) collective-permute-start(bf16[1,48,768]{2,1,0:T(8,128)(2,1)S(1)} %bitcast.56), channel_id=1, source_target_pairs={{0,16},{4,20},{8,24},{12,28},{16,0},{20,4},{24,8},{28,12},{1,17},{... | collective-permute-start | bytes 221192 | tf_op jit(solution)/shard_map/ppermute | solution.py:77
  29.2 10.1 %collective-permute-start = (bf16[1,64,768]{2,1,0:T(8,128)(2,1)S(1)}, bf16[1,64,768]{2,1,0:T(8,128)(2,1)S(1)}, u32[]{:S(2)}, u32[]{:S(2)}) collective-permute-start(bf16[1,64,768]{2,1,0:T(8,128)(2,1)S(1)} %bitcast.51), channel_id=1, source_target_pairs={{0,8},{4,12},{8,0},{12,4},{16,24},{20,28},{24,16},{28,20},{1,9},{5... | collective-permute-start | bytes 294920 | tf_op jit(solution)/shard_map/ppermute | solution.py:77
  29.6 13.2 %collective-permute-start.1 = (bf16[1,64,768]{2,1,0:T(8,128)(2,1)S(1)}, bf16[1,64,768]{2,1,0:T(8,128)(2,1)S(1)}, u32[]{:S(2)}, u32[]{:S(2)}) collective-permute-start(bf16[1,64,768]{2,1,0:T(8,128)(2,1)S(1)} %bitcast.52), channel_id=1, source_target_pairs={{0,16},{4,20},{8,24},{12,28},{16,0},{20,4},{24,8},{28,12},{1,17},{... | collective-permute-start | bytes 294920 | tf_op jit(solution)/shard_map/ppermute | solution.py:77
  35.0 10.2 %collective-permute-start.31 = (bf16[2,96,384]{2,1,0:T(8,128)(2,1)S(1)}, bf16[2,96,384]{2,1,0:T(8,128)(2,1)S(1)}, u32[]{:S(2)}, u32[]{:S(2)}) collective-permute-start(bf16[2,96,384]{2,1,0:T(8,128)(2,1)S(1)} %pad_maximum_fusion.5), channel_id=1, source_target_pairs={{0,8},{4,12},{8,0},{12,4},{16,24},{20,28},{24,16},{28,20},{1,9},{5... | collective-permute-start | bytes 442376 | tf_op jit(solution)/shard_map/ppermute | solution.py:77
  35.4 18.5 %collective-permute-start.32 = (bf16[2,96,384]{2,1,0:T(8,128)(2,1)S(1)}, bf16[2,96,384]{2,1,0:T(8,128)(2,1)S(1)}, u32[]{:S(2)}, u32[]{:S(2)}) collective-permute-start(bf16[2,96,384]{2,1,0:T(8,128)(2,1)S(1)} %pad_maximum_fusion.5), channel_id=1, source_target_pairs={{0,16},{4,20},{8,24},{12,28},{16,0},{20,4},{24,8},{28,12},{1,17},{... | collective-permute-start | bytes 442376 | tf_op jit(solution)/shard_map/ppermute | solution.py:77
  39.3 18.1 %collective-permute-start.33 = (bf16[2,96,384]{2,1,0:T(8,128)(2,1)S(1)}, bf16[2,96,384]{2,1,0:T(8,128)(2,1)S(1)}, u32[]{:S(2)}, u32[]{:S(2)}) collective-permute-start(bf16[2,96,384]{2,1,0:T(8,128)(2,1)S(1)} %pad_maximum_fusion.5), channel_id=1, source_target_pairs={{0,24},{4,28},{8,16},{12,20},{16,8},{20,12},{24,0},{28,4},{1,25},{... | collective-permute-start | bytes 442376 | tf_op jit(solution)/shard_map/ppermute | solution.py:77
  43.4 12.3 %collective-permute-start.3 = (bf16[4,64,768]{2,1,0:T(8,128)(2,1)S(1)}, bf16[4,64,768]{2,1,0:T(8,128)(2,1)S(1)}, u32[]{:S(2)}, u32[]{:S(2)}) collective-permute-start(bf16[4,64,768]{2,1,0:T(8,128)(2,1)S(1)} %pad_maximum_fusion), channel_id=1, source_target_pairs={{0,4},{4,0},{8,12},{12,8},{16,20},{20,16},{24,28},{28,24},{1,5},{5... | collective-permute-start | bytes 1179656 | tf_op jit(solution)/shard_map/ppermute | solution.py:77
  45.2 13.8 %collective-permute-start.25 = (bf16[2,96,384]{2,1,0:T(8,128)(2,1)S(1)}, bf16[2,96,384]{2,1,0:T(8,128)(2,1)S(1)}, u32[]{:S(2)}, u32[]{:S(2)}) collective-permute-start(bf16[2,96,384]{2,1,0:T(8,128)(2,1)S(1)} %pad_maximum_fusion.4), channel_id=1, source_target_pairs={{0,8},{4,12},{8,0},{12,4},{16,24},{20,28},{24,16},{28,20},{1,9},{5... | collective-permute-start | bytes 442376 | tf_op jit(solution)/shard_map/ppermute | solution.py:77
  51.8 13.1 %collective-permute-start.26 = (bf16[2,96,384]{2,1,0:T(8,128)(2,1)S(1)}, bf16[2,96,384]{2,1,0:T(8,128)(2,1)S(1)}, u32[]{:S(2)}, u32[]{:S(2)}) collective-permute-start(bf16[2,96,384]{2,1,0:T(8,128)(2,1)S(1)} %pad_maximum_fusion.4), channel_id=1, source_target_pairs={{0,16},{4,20},{8,24},{12,28},{16,0},{20,4},{24,8},{28,12},{1,17},{... | collective-permute-start | bytes 442376 | tf_op jit(solution)/shard_map/ppermute | solution.py:77
  53.9 14.8 %collective-permute-start.10 = (bf16[8,48,768]{2,1,0:T(8,128)(2,1)S(1)}, bf16[8,48,768]{2,1,0:T(8,128)(2,1)S(1)}, u32[]{:S(2)}, u32[]{:S(2)}) collective-permute-start(bf16[8,48,768]{2,1,0:T(8,128)(2,1)S(1)} %get-tuple-element.232), channel_id=1, source_target_pairs={{0,4},{4,0},{8,12},{12,8},{16,20},{20,16},{24,28},{28,24},{1,5},{5... | collective-permute-start | bytes 1769480 | tf_op jit(solution)/shard_map/ppermute | solution.py:77
  55.7 13.9 %collective-permute-start.27 = (bf16[2,96,384]{2,1,0:T(8,128)(2,1)S(1)}, bf16[2,96,384]{2,1,0:T(8,128)(2,1)S(1)}, u32[]{:S(2)}, u32[]{:S(2)}) collective-permute-start(bf16[2,96,384]{2,1,0:T(8,128)(2,1)S(1)} %pad_maximum_fusion.4), channel_id=1, source_target_pairs={{0,24},{4,28},{8,16},{12,20},{16,8},{20,12},{24,0},{28,4},{1,25},{... | collective-permute-start | bytes 442376 | tf_op jit(solution)/shard_map/ppermute | solution.py:77
  57.4 27.1 %collective-permute-start.4 = (bf16[8,64,768]{2,1,0:T(8,128)(2,1)S(1)}, bf16[8,64,768]{2,1,0:T(8,128)(2,1)S(1)}, u32[]{:S(2)}, u32[]{:S(2)}) collective-permute-start(bf16[8,64,768]{2,1,0:T(8,128)(2,1)S(1)} %get-tuple-element.222), channel_id=1, source_target_pairs={{0,2},{1,3},{2,0},{3,1},{4,6},{5,7},{6,4},{7,5},{8,10},{9,11},{10,... | collective-permute-start | bytes 2359304 | tf_op jit(solution)/shard_map/ppermute | solution.py:77
  59.0 22.5 %collective-permute-start.21 = (bf16[4,48,768]{2,1,0:T(8,128)(2,1)S(1)}, bf16[4,48,768]{2,1,0:T(8,128)(2,1)S(1)}, u32[]{:S(2)}, u32[]{:S(2)}) collective-permute-start(bf16[4,48,768]{2,1,0:T(8,128)(2,1)S(1)} %pad_maximum_fusion.3), channel_id=1, source_target_pairs={{0,2},{1,3},{2,0},{3,1},{4,6},{5,7},{6,4},{7,5},{8,10},{9,11},{10,... | collective-permute-start | bytes 884744 | tf_op jit(solution)/shard_map/ppermute | solution.py:77
  64.9 18.2 %collective-permute-start.15 = (bf16[4,48,768]{2,1,0:T(8,128)(2,1)S(1)}, bf16[4,48,768]{2,1,0:T(8,128)(2,1)S(1)}, u32[]{:S(2)}, u32[]{:S(2)}) collective-permute-start(bf16[4,48,768]{2,1,0:T(8,128)(2,1)S(1)} %pad_maximum_fusion.2), channel_id=1, source_target_pairs={{0,4},{4,0},{8,12},{12,8},{16,20},{20,16},{24,28},{28,24},{1,5},{5... | collective-permute-start | bytes 884744 | tf_op jit(solution)/shard_map/ppermute | solution.py:77
  68.7 19.0 %collective-permute-start.34 = (bf16[8,96,384]{2,1,0:T(8,128)(2,1)S(1)}, bf16[8,96,384]{2,1,0:T(8,128)(2,1)S(1)}, u32[]{:S(2)}, u32[]{:S(2)}) collective-permute-start(bf16[8,96,384]{2,1,0:T(8,128)(2,1)S(1)} %get-tuple-element.234), channel_id=1, source_target_pairs={{0,4},{4,0},{8,12},{12,8},{16,20},{20,16},{24,28},{28,24},{1,5},{5... | collective-permute-start | bytes 1769480 | tf_op jit(solution)/shard_map/ppermute | solution.py:77
  69.6 37.8 %collective-permute-start.11 = (bf16[16,48,768]{2,1,0:T(8,128)(2,1)S(1)}, bf16[16,48,768]{2,1,0:T(8,128)(2,1)S(1)}, u32[]{:S(2)}, u32[]{:S(2)}) collective-permute-start(bf16[16,48,768]{2,1,0:T(8,128)(2,1)S(1)} %constant_dynamic-update-slice_fusion.16.refs_2_), channel_id=1, source_target_pairs={{0,1},{1,0},{2,3},{3,2},{4,5},{5,4},{6,7},{7,6},{8,9},{9,8},{10,11... | collective-permute-start | bytes 3538952 | tf_op jit(solution)/shard_map/ppermute | solution.py:77
  81.5 16.3 %collective-permute-start.28 = (bf16[8,96,384]{2,1,0:T(8,128)(2,1)S(1)}, bf16[8,96,384]{2,1,0:T(8,128)(2,1)S(1)}, u32[]{:S(2)}, u32[]{:S(2)}) collective-permute-start(bf16[8,96,384]{2,1,0:T(8,128)(2,1)S(1)} %get-tuple-element.240), channel_id=1, source_target_pairs={{0,2},{1,3},{2,0},{3,1},{4,6},{5,7},{6,4},{7,5},{8,10},{9,11},{10,... | collective-permute-start | bytes 1769480 | tf_op jit(solution)/shard_map/ppermute | solution.py:77
  83.1 15.7 %collective-permute-start.22 = (bf16[8,48,768]{2,1,0:T(8,128)(2,1)S(1)}, bf16[8,48,768]{2,1,0:T(8,128)(2,1)S(1)}, u32[]{:S(2)}, u32[]{:S(2)}) collective-permute-start(bf16[8,48,768]{2,1,0:T(8,128)(2,1)S(1)} %get-tuple-element.228), channel_id=1, source_target_pairs={{0,4},{4,0},{8,12},{12,8},{16,20},{20,16},{24,28},{28,24},{1,5},{5... | collective-permute-start | bytes 1769480 | tf_op jit(solution)/shard_map/ppermute | solution.py:77
  84.6 22.0 %collective-permute-start.16 = (bf16[8,48,768]{2,1,0:T(8,128)(2,1)S(1)}, bf16[8,48,768]{2,1,0:T(8,128)(2,1)S(1)}, u32[]{:S(2)}, u32[]{:S(2)}) collective-permute-start(bf16[8,48,768]{2,1,0:T(8,128)(2,1)S(1)} %get-tuple-element.230), channel_id=1, source_target_pairs={{0,2},{1,3},{2,0},{3,1},{4,6},{5,7},{6,4},{7,5},{8,10},{9,11},{10,... | collective-permute-start | bytes 1769480 | tf_op jit(solution)/shard_map/ppermute | solution.py:77
  87.6 22.1 %collective-permute-start.5 = (bf16[16,64,768]{2,1,0:T(8,128)(2,1)S(1)}, bf16[16,64,768]{2,1,0:T(8,128)(2,1)}, u32[]{:S(2)}, u32[]{:S(2)}) collective-permute-start(bf16[16,64,768]{2,1,0:T(8,128)(2,1)S(1)} %constant_dynamic-update-slice_fusion.5.refs_0_), channel_id=1, source_target_pairs={{0,1},{1,0},{2,3},{3,2},{4,5},{5,4},{6,7},{7,6},{8,9},{9,8},{10,11... | collective-permute-start | bytes 4718600 | tf_op jit(solution)/shard_map/ppermute | solution.py:77
  97.8 46.8 %collective-permute-start.35 = (bf16[16,96,384]{2,1,0:T(8,128)(2,1)}, bf16[16,96,384]{2,1,0:T(8,128)(2,1)}, u32[]{:S(2)}, u32[]{:S(2)}) collective-permute-start(bf16[16,96,384]{2,1,0:T(8,128)(2,1)} %constant_dynamic-update-slice_fusion.60.refs_6_), channel_id=1, source_target_pairs={{0,1},{1,0},{2,3},{3,2},{4,5},{5,4},{6,7},{7,6},{8,9},{9,8},{10,11... | collective-permute-start | bytes 3538952 | tf_op jit(solution)/shard_map/ppermute | solution.py:77
  98.8 45.9 %collective-permute-start.29 = (bf16[16,96,384]{2,1,0:T(8,128)(2,1)}, bf16[16,96,384]{2,1,0:T(8,128)(2,1)}, u32[]{:S(2)}, u32[]{:S(2)}) collective-permute-start(bf16[16,96,384]{2,1,0:T(8,128)(2,1)} %constant_dynamic-update-slice_fusion.49.refs_4_), channel_id=1, source_target_pairs={{0,1},{1,0},{2,3},{3,2},{4,5},{5,4},{6,7},{7,6},{8,9},{9,8},{10,11... | collective-permute-start | bytes 3538952 | tf_op jit(solution)/shard_map/ppermute | solution.py:77
  106.5 38.1 %collective-permute-start.23 = (bf16[16,48,768]{2,1,0:T(8,128)(2,1)}, bf16[16,48,768]{2,1,0:T(8,128)(2,1)}, u32[]{:S(2)}, u32[]{:S(2)}) collective-permute-start(bf16[16,48,768]{2,1,0:T(8,128)(2,1)} %constant_dynamic-update-slice_fusion.38.refs_2_), channel_id=1, source_target_pairs={{0,1},{1,0},{2,3},{3,2},{4,5},{5,4},{6,7},{7,6},{8,9},{9,8},{10,11... | collective-permute-start | bytes 3538952 | tf_op jit(solution)/shard_map/ppermute | solution.py:77
  108.5 36.2 %collective-permute-start.17 = (bf16[16,48,768]{2,1,0:T(8,128)(2,1)}, bf16[16,48,768]{2,1,0:T(8,128)(2,1)}, u32[]{:S(2)}, u32[]{:S(2)}) collective-permute-start(bf16[16,48,768]{2,1,0:T(8,128)(2,1)} %constant_dynamic-update-slice_fusion.27.refs_0_), channel_id=1, source_target_pairs={{0,1},{1,0},{2,3},{3,2},{4,5},{5,4},{6,7},{7,6},{8,9},{9,8},{10,11... | collective-permute-start | bytes 3538952 | tf_op jit(solution)/shard_map/ppermute | solution.py:77
  186.2 35.3 %collective-permute-start.54 = (bf16[16,48,768]{2,1,0:T(8,128)(2,1)S(1)}, bf16[16,48,768]{2,1,0:T(8,128)(2,1)}, u32[]{:S(2)}, u32[]{:S(2)}) collective-permute-start(bf16[16,48,768]{2,1,0:T(8,128)(2,1)S(1)} %get-tuple-element.114), channel_id=1, source_target_pairs={{0,1},{1,0},{2,3},{3,2},{4,5},{5,4},{6,7},{7,6},{8,9},{9,8},{10,11... | collective-permute-start | bytes 3538952 | tf_op jit(solution)/shard_map/ppermute | solution.py:77
  186.2 37.2 %collective-permute-start.48 = (bf16[16,48,768]{2,1,0:T(8,128)(2,1)S(1)}, bf16[16,48,768]{2,1,0:T(8,128)(2,1)}, u32[]{:S(2)}, u32[]{:S(2)}) collective-permute-start(bf16[16,48,768]{2,1,0:T(8,128)(2,1)S(1)} %get-tuple-element.112), channel_id=1, source_target_pairs={{0,1},{1,0},{2,3},{3,2},{4,5},{5,4},{6,7},{7,6},{8,9},{9,8},{10,11... | collective-permute-start | bytes 3538952 | tf_op jit(solution)/shard_map/ppermute | solution.py:77
  223.5 16.3 %collective-permute-start.55 = (bf16[8,48,768]{2,1,0:T(8,128)(2,1)S(1)}, bf16[8,48,768]{2,1,0:T(8,128)(2,1)S(1)}, u32[]{:S(2)}, u32[]{:S(2)}) collective-permute-start(bf16[8,48,768]{2,1,0:T(8,128)(2,1)S(1)} %get-tuple-element.181), channel_id=1, source_target_pairs={{0,4},{4,0},{8,12},{12,8},{16,20},{20,16},{24,28},{28,24},{1,5},{5... | collective-permute-start | bytes 1769480 | tf_op jit(solution)/shard_map/ppermute | solution.py:77
  225.8 16.3 %collective-permute-start.49 = (bf16[8,48,768]{2,1,0:T(8,128)(2,1)S(1)}, bf16[8,48,768]{2,1,0:T(8,128)(2,1)S(1)}, u32[]{:S(2)}, u32[]{:S(2)}) collective-permute-start(bf16[8,48,768]{2,1,0:T(8,128)(2,1)S(1)} %get-tuple-element.183), channel_id=1, source_target_pairs={{0,2},{1,3},{2,0},{3,1},{4,6},{5,7},{6,4},{7,5},{8,10},{9,11},{10,... | collective-permute-start | bytes 1769480 | tf_op jit(solution)/shard_map/ppermute | solution.py:77
  226.9 38.0 %collective-permute-start.43 = (bf16[8,48,768]{2,1,0:T(8,128)(2,1)S(1)}, bf16[8,48,768]{2,1,0:T(8,128)(2,1)S(1)}, u32[]{:S(2)}, u32[]{:S(2)}) collective-permute-start(bf16[8,48,768]{2,1,0:T(8,128)(2,1)S(1)} %get-tuple-element.185), channel_id=1, source_target_pairs={{0,4},{4,0},{8,12},{12,8},{16,20},{20,16},{24,28},{28,24},{1,5},{5... | collective-permute-start | bytes 1769480 | tf_op jit(solution)/shard_map/ppermute | solution.py:77
  229.6 34.5 %collective-permute-start.67 = (bf16[8,96,384]{2,1,0:T(8,128)(2,1)S(1)}, bf16[8,96,384]{2,1,0:T(8,128)(2,1)S(1)}, u32[]{:S(2)}, u32[]{:S(2)}) collective-permute-start(bf16[8,96,384]{2,1,0:T(8,128)(2,1)S(1)} %get-tuple-element.187), channel_id=1, source_target_pairs={{0,4},{4,0},{8,12},{12,8},{16,20},{20,16},{24,28},{28,24},{1,5},{5... | collective-permute-start | bytes 1769480 | tf_op jit(solution)/shard_map/ppermute | solution.py:77
  230.6 35.0 %collective-permute-start.61 = (bf16[8,96,384]{2,1,0:T(8,128)(2,1)S(1)}, bf16[8,96,384]{2,1,0:T(8,128)(2,1)S(1)}, u32[]{:S(2)}, u32[]{:S(2)}) collective-permute-start(bf16[8,96,384]{2,1,0:T(8,128)(2,1)S(1)} %get-tuple-element.189), channel_id=1, source_target_pairs={{0,2},{1,3},{2,0},{3,1},{4,6},{5,7},{6,4},{7,5},{8,10},{9,11},{10,... | collective-permute-start | bytes 1769480 | tf_op jit(solution)/shard_map/ppermute | solution.py:77
  239.7 61.9 %collective-permute-start.37 = (bf16[8,64,768]{2,1,0:T(8,128)(2,1)S(1)}, bf16[8,64,768]{2,1,0:T(8,128)(2,1)S(1)}, u32[]{:S(2)}, u32[]{:S(2)}) collective-permute-start(bf16[8,64,768]{2,1,0:T(8,128)(2,1)S(1)} %get-tuple-element.179), channel_id=1, source_target_pairs={{0,2},{1,3},{2,0},{3,1},{4,6},{5,7},{6,4},{7,5},{8,10},{9,11},{10,... | collective-permute-start | bytes 2359304 | tf_op jit(solution)/shard_map/ppermute | solution.py:77
  242.1 55.5 %collective-permute-start.56 = (bf16[4,48,768]{2,1,0:T(8,128)(2,1)S(1)}, bf16[4,48,768]{2,1,0:T(8,128)(2,1)S(1)}, u32[]{:S(2)}, u32[]{:S(2)}) collective-permute-start(bf16[4,48,768]{2,1,0:T(8,128)(2,1)S(1)} %get-tuple-element.193), channel_id=1, source_target_pairs={{0,2},{1,3},{2,0},{3,1},{4,6},{5,7},{6,4},{7,5},{8,10},{9,11},{10,... | collective-permute-start | bytes 884744 | tf_op jit(solution)/shard_map/ppermute | solution.py:77
  264.1 37.8 %collective-permute-start.50 = (bf16[4,48,768]{2,1,0:T(8,128)(2,1)S(1)}, bf16[4,48,768]{2,1,0:T(8,128)(2,1)S(1)}, u32[]{:S(2)}, u32[]{:S(2)}) collective-permute-start(bf16[4,48,768]{2,1,0:T(8,128)(2,1)S(1)} %get-tuple-element.195), channel_id=1, source_target_pairs={{0,4},{4,0},{8,12},{12,8},{16,20},{20,16},{24,28},{28,24},{1,5},{5... | collective-permute-start | bytes 884744 | tf_op jit(solution)/shard_map/ppermute | solution.py:77
  280.6 21.5 %collective-permute-start.44 = (bf16[4,48,768]{2,1,0:T(8,128)(2,1)S(1)}, bf16[4,48,768]{2,1,0:T(8,128)(2,1)S(1)}, u32[]{:S(2)}, u32[]{:S(2)}) collective-permute-start(bf16[4,48,768]{2,1,0:T(8,128)(2,1)S(1)} %get-tuple-element.197), channel_id=1, source_target_pairs={{0,2},{1,3},{2,0},{3,1},{4,6},{5,7},{6,4},{7,5},{8,10},{9,11},{10,... | collective-permute-start | bytes 884744 | tf_op jit(solution)/shard_map/ppermute | solution.py:77
  301.9 10.3 %collective-permute-start.38 = (bf16[4,64,768]{2,1,0:T(8,128)(2,1)S(1)}, bf16[4,64,768]{2,1,0:T(8,128)(2,1)S(1)}, u32[]{:S(2)}, u32[]{:S(2)}) collective-permute-start(bf16[4,64,768]{2,1,0:T(8,128)(2,1)S(1)} %get-tuple-element.191), channel_id=1, source_target_pairs={{0,4},{4,0},{8,12},{12,8},{16,20},{20,16},{24,28},{28,24},{1,5},{5... | collective-permute-start | bytes 1179656 | tf_op jit(solution)/shard_map/ppermute | solution.py:77
  302.1 10.1 %collective-permute-start.58 = (bf16[1,48,768]{2,1,0:T(8,128)(2,1)S(1)}, bf16[1,48,768]{2,1,0:T(8,128)(2,1)S(1)}, u32[]{:S(2)}, u32[]{:S(2)}) collective-permute-start(bf16[1,48,768]{2,1,0:T(8,128)(2,1)S(1)} %get-tuple-element.211), channel_id=1, source_target_pairs={{0,16},{4,20},{8,24},{12,28},{16,0},{20,4},{24,8},{28,12},{1,17},{... | collective-permute-start | bytes 221192 | tf_op jit(solution)/shard_map/ppermute | solution.py:77
  306.7 10.1 %collective-permute-start.51 = (bf16[1,48,768]{2,1,0:T(8,128)(2,1)S(1)}, bf16[1,48,768]{2,1,0:T(8,128)(2,1)S(1)}, u32[]{:S(2)}, u32[]{:S(2)}) collective-permute-start(bf16[1,48,768]{2,1,0:T(8,128)(2,1)S(1)} %get-tuple-element.216), channel_id=1, source_target_pairs={{0,8},{4,12},{8,0},{12,4},{16,24},{20,28},{24,16},{28,20},{1,9},{5... | collective-permute-start | bytes 221192 | tf_op jit(solution)/shard_map/ppermute | solution.py:77
  308.4 10.6 %collective-permute-start.52 = (bf16[1,48,768]{2,1,0:T(8,128)(2,1)S(1)}, bf16[1,48,768]{2,1,0:T(8,128)(2,1)S(1)}, u32[]{:S(2)}, u32[]{:S(2)}) collective-permute-start(bf16[1,48,768]{2,1,0:T(8,128)(2,1)S(1)} %get-tuple-element.215), channel_id=1, source_target_pairs={{0,16},{4,20},{8,24},{12,28},{16,0},{20,4},{24,8},{28,12},{1,17},{... | collective-permute-start | bytes 221192 | tf_op jit(solution)/shard_map/ppermute | solution.py:77
  312.3 15.1 %collective-permute-start.40 = (bf16[1,64,768]{2,1,0:T(8,128)(2,1)S(1)}, bf16[1,64,768]{2,1,0:T(8,128)(2,1)S(1)}, u32[]{:S(2)}, u32[]{:S(2)}) collective-permute-start(bf16[1,64,768]{2,1,0:T(8,128)(2,1)S(1)} %get-tuple-element.207), channel_id=1, source_target_pairs={{0,16},{4,20},{8,24},{12,28},{16,0},{20,4},{24,8},{28,12},{1,17},{... | collective-permute-start | bytes 294920 | tf_op jit(solution)/shard_map/ppermute | solution.py:77
  316.8 10.7 %collective-permute-start.41 = (bf16[1,64,768]{2,1,0:T(8,128)(2,1)S(1)}, bf16[1,64,768]{2,1,0:T(8,128)(2,1)S(1)}, u32[]{:S(2)}, u32[]{:S(2)}) collective-permute-start(bf16[1,64,768]{2,1,0:T(8,128)(2,1)S(1)} %get-tuple-element.206), channel_id=1, source_target_pairs={{0,24},{4,28},{8,16},{12,20},{16,8},{20,12},{24,0},{28,4},{1,25},{... | collective-permute-start | bytes 294920 | tf_op jit(solution)/shard_map/ppermute | solution.py:77
  330.3 10.9 %all-to-all-start = ((f32[32,1,128]{2,1,0:T(1,128)}), f32[32,1,128]{2,1,0:T(1,128)S(1)}, u32[]{:S(2)}, u32[]{:S(2)}) async-start(f32[32,1,128]{2,1,0:T(1,128)} %broadcast_in_dim.33), calls=%async_computation | async-start | bytes 32768 | tf_op jit(solution)/shard_map/all_to_all | solution.py:913
  (77 other events, 481.1 us)
